TPU v7x, 32 devices: a whole 2x2x4 slice. The times are simulated.
32 devices in a mesh: seq: 8 (over y, x, core), enc: 4 (over z).
Axes of the slice: x: 2, y: 2, z: 4, core: 2. Of those that a mesh axis runs over, the one named last changes fastest.
Arguments:
- queries: bfloat16 [1024, 8192], P('seq', 'enc'), may hold values from -63 to 63
- image_key_value: bfloat16 [2, 32, 1601, 1024], P(None, ('seq', 'enc')), may hold values from -16 to 16
- image_spans: int32 [8, 2], replicated, may hold values from 0 to 1024, as said below
- tile_counts: int32 [8], replicated, may hold values from 1 to 4
- cross_gate: float32 [1], replicated, may hold values from 0.2 to 2
- grad_out: bfloat16 [1024, 8192], P('seq', 'enc'), may hold values from -6 to 6
Outputs:
- attended: bfloat16 [1024, 8192], P('seq', 'enc')
- grad_queries: bfloat16 [1024, 8192], P('seq', 'enc')
- grad_image_kv: bfloat16 [2, 32, 1601, 1024], P(None, ('seq', 'enc'))
Inputs may be any that keep to these rules, and one draw needn't show every extreme that they name: `image_spans`: image m owns tiles 4 m to 4 m + 3. Its span starts in text shard m (positions (m) * 128 to (m) * 128 + 127), starts do not fall from one image to the next within a shard, and each span holds 1 to 128 positions.
All inputs are finite; a program needn't handle non-finite values.
Results may differ from a plain program's by a relative error of at most 0.0062.
Values may be sent and summed in bfloat16 or wider, within the bound.
No kernel may reach another device: no remote copies, remote signals or barrier semaphores. Data moves between devices by JAX's collectives and lax.ppermute only.
A program may use at most 128 MiB of HBM per device.

v0:
```python
import jax
import jax.numpy as jnp
from jax import lax
from jax.sharding import PartitionSpec as P

HEAD_SIZE = 128
TILES = 4


NEG_FILL = -1e30


def shifted(shard, axis, by):
    devices = lax.axis_size(axis)
    pairs = [(i, i + by) for i in range(devices) if 0 <= i + by < devices]
    return lax.ppermute(shard, axis, pairs)


def visible_rows(image_spans, tile_counts, first_tile, tile_total, first_text, text_rows):
    image_total = image_spans.shape[0]
    tile_ids = first_tile + jnp.arange(tile_total, dtype=jnp.int32)
    image_ids = jnp.floor_divide(tile_ids, TILES)
    slot_ids = tile_ids - image_ids * TILES
    lookup = (image_ids[:, None] == jnp.arange(image_total, dtype=jnp.int32)[None, :]).astype(
        jnp.int32
    )
    starts = jnp.sum(lookup * image_spans[:, 0][None, :], axis=1)
    span_ends = jnp.sum(lookup * image_spans[:, 1][None, :], axis=1)
    in_use = jnp.sum(lookup * tile_counts[None, :], axis=1)
    usable = (tile_ids >= 0) & (slot_ids < in_use)
    positions = first_text + jnp.arange(text_rows, dtype=jnp.int32)
    return (
        usable[None, :]
        & (positions[:, None] >= starts[None, :])
        & (positions[:, None] < span_ends[None, :])
    )


def keep_state(stats_now):
    return stats_now


def score_block(query_head, key_tile, softmax_scale):
    return (
        jnp.einsum("tgd,jd->tgj", query_head, key_tile, preferred_element_type=jnp.float32)
        * softmax_scale
    )


def forward_tiles(query_heads, key_tiles, value_tiles, visible, softmax_scale):
    active = jnp.any(visible, axis=0)
    columns = visible.T
    text_rows, local_heads, head_groups, head_dim = query_heads.shape
    outputs = []
    log_sums = []
    for head_index in range(local_heads):
        query_head = query_heads[:, head_index]
        head_keys = key_tiles[:, :, head_index]
        head_values = value_tiles[:, :, head_index]

        def online_step(carried, tile_item):
            key_tile, value_tile, column, tile_live = tile_item

            def online_update(state):
                run_max, run_total, run_out = state
                scores = score_block(query_head, key_tile, softmax_scale)
                row_mask = column[:, None, None]
                tile_max = jnp.max(jnp.where(row_mask, scores, NEG_FILL), axis=2)
                new_max = jnp.maximum(run_max, tile_max)
                factor = jnp.exp(run_max - new_max)
                probs = jnp.where(row_mask, jnp.exp(scores - new_max[:, :, None]), 0.0)
                new_total = run_total * factor + jnp.sum(probs, axis=2)
                new_out = run_out * factor[:, :, None] + jnp.einsum(
                    "tgj,jd->tgd",
                    probs.astype(jnp.bfloat16),
                    value_tile,
                    preferred_element_type=jnp.float32,
                )
                return (new_max, new_total, new_out)

            return (lax.cond(tile_live, online_update, keep_state, carried), None)

        starting_state = (
            jnp.full((text_rows, head_groups), NEG_FILL, jnp.float32),
            jnp.zeros((text_rows, head_groups), jnp.float32),
            jnp.zeros((text_rows, head_groups, head_dim), jnp.float32),
        )
        (run_max, run_total, run_out), unused = lax.scan(
            online_step, starting_state, (head_keys, head_values, columns, active)
        )
        seen = run_total > 0.0
        safe_total = jnp.where(seen, run_total, 1.0)
        log_total = jnp.where(seen, run_max + jnp.log(safe_total), 0.0)
        mixed_head = jnp.where(seen[:, :, None], run_out / safe_total[:, :, None], 0.0)
        outputs.append(mixed_head)
        log_sums.append(log_total)
    return (jnp.stack(outputs, 1), jnp.stack(log_sums, 1))


def backward_tiles(
    query_heads, grad_heads, log_totals, row_deltas, key_tiles, value_tiles, visible, softmax_scale
):
    active = jnp.any(visible, axis=0)
    columns = visible.T
    text_rows, local_heads, head_groups, head_dim = query_heads.shape
    query_grads = []
    key_grads = []
    value_grads = []
    for head_index in range(local_heads):
        query_head = query_heads[:, head_index]
        grad_head = grad_heads[:, head_index]
        log_total = log_totals[:, head_index]
        row_delta = row_deltas[:, head_index]
        head_keys = key_tiles[:, :, head_index]
        head_values = value_tiles[:, :, head_index]

        def grad_step(carried, tile_item):
            key_tile, value_tile, column, tile_live = tile_item

            def grad_update(running):
                scores = score_block(query_head, key_tile, softmax_scale)
                weights = jnp.where(
                    column[:, None, None], jnp.exp(scores - log_total[:, :, None]), 0.0
                )
                weights_low = weights.astype(jnp.bfloat16)
                grad_weights = jnp.einsum(
                    "tgd,jd->tgj", grad_head, value_tile, preferred_element_type=jnp.float32
                )
                grad_scores = (weights * (grad_weights - row_delta[:, :, None])).astype(
                    jnp.bfloat16
                )
                new_running = (
                    running
                    + jnp.einsum(
                        "tgj,jd->tgd", grad_scores, key_tile, preferred_element_type=jnp.float32
                    )
                    * softmax_scale
                )
                key_term = (
                    jnp.einsum(
                        "tgj,tgd->jd", grad_scores, query_head, preferred_element_type=jnp.float32
                    )
                    * softmax_scale
                ).astype(jnp.bfloat16)
                value_term = jnp.einsum(
                    "tgj,tgd->jd", weights_low, grad_head, preferred_element_type=jnp.float32
                ).astype(jnp.bfloat16)
                return (new_running, (key_term, value_term))

            def passed(running):
                zero_rows = jnp.zeros(key_tile.shape, jnp.bfloat16)
                return (running, (zero_rows, zero_rows))

            return lax.cond(tile_live, grad_update, passed, carried)

        query_grad, (key_term, value_term) = lax.scan(
            grad_step,
            jnp.zeros((text_rows, head_groups, head_dim), jnp.float32),
            (head_keys, head_values, columns, active),
        )
        query_grads.append(query_grad)
        key_grads.append(key_term)
        value_grads.append(value_term)
    return (jnp.stack(query_grads, 1), jnp.stack(key_grads, 2), jnp.stack(value_grads, 2))


def shards(queries, image_key_value, image_spans, tile_counts, cross_gate, grad_out):
    seq_index = lax.axis_index("seq")
    enc_total = lax.axis_size("enc")
    text_rows = queries.shape[0]
    tile_tokens = image_key_value.shape[2]
    local_heads = image_key_value.shape[3] // (enc_total * HEAD_SIZE)
    head_groups = queries.shape[1] // (local_heads * HEAD_SIZE)
    width = local_heads * HEAD_SIZE
    softmax_scale = HEAD_SIZE ** (-0.5)
    split_kv = image_key_value.reshape(2, 1, tile_tokens, enc_total, width)
    own_rows = lax.all_to_all(split_kv, "enc", split_axis=3, concat_axis=1, tiled=True)
    prev_rows = shifted(own_rows, "seq", 1)
    reach = jnp.concatenate([prev_rows, own_rows], 1).reshape(
        2, 2 * enc_total, tile_tokens, local_heads, HEAD_SIZE
    )
    key_tiles = reach[0]
    value_tiles = reach[1]
    visible = visible_rows(
        image_spans,
        tile_counts,
        (seq_index - 1) * enc_total,
        2 * enc_total,
        seq_index * text_rows,
        text_rows,
    )
    query_heads = queries.reshape(text_rows, local_heads, head_groups, HEAD_SIZE)
    mixed, log_totals = forward_tiles(query_heads, key_tiles, value_tiles, visible, softmax_scale)
    gate_value = jnp.tanh(cross_gate[0])
    attended = (
        (gate_value * mixed)
        .reshape(text_rows, local_heads * head_groups * HEAD_SIZE)
        .astype(jnp.bfloat16)
    )
    gradient_blended = (gate_value * grad_out.astype(jnp.float32)).astype(jnp.bfloat16)
    grad_heads = gradient_blended.reshape(text_rows, local_heads, head_groups, HEAD_SIZE)
    row_deltas = jnp.sum(grad_heads.astype(jnp.float32) * mixed, axis=3)
    query_grad, key_term, value_term = backward_tiles(
        query_heads,
        grad_heads,
        log_totals,
        row_deltas,
        key_tiles,
        value_tiles,
        visible,
        softmax_scale,
    )
    terms = jnp.stack([key_term, value_term], 0).reshape(2, 2 * enc_total, tile_tokens, 1, width)
    later_terms = shifted(terms[:, :enc_total], "seq", -1)
    row_grads = (terms[:, enc_total:].astype(jnp.float32) + later_terms.astype(jnp.float32)).astype(
        jnp.bfloat16
    )
    home_grads = lax.all_to_all(row_grads, "enc", split_axis=1, concat_axis=3, tiled=True)
    grad_image_kv = home_grads.reshape(2, 1, tile_tokens, enc_total * width)
    grad_queries = query_grad.reshape(text_rows, local_heads * head_groups * HEAD_SIZE).astype(
        jnp.bfloat16
    )
    return (attended, grad_queries, grad_image_kv)


def solution(mesh):
    in_specs = (
        P("seq", "enc"),
        P(None, ("seq", "enc"), None, None),
        P(),
        P(),
        P(),
        P("seq", "enc"),
    )
    out_specs = (P("seq", "enc"), P("seq", "enc"), P(None, ("seq", "enc"), None, None))
    return jax.shard_map(shards, mesh=mesh, in_specs=in_specs, out_specs=out_specs, check_vma=False)
```

profile of v0, /device:TPU:3, one launch (start us, length us, event | category | flops | bytes accessed | tf_op | source)
XLA Modules:
  0.0 857.2 jit_solution(13155390868984679756)
XLA Ops:
  0.6 17.4 %copy.178 = bf16[2,1,1601,1024]{2,3,0,1:T(8,128)(2,1)} copy(bf16[2,1,1601,1024]{3,0,2,1:T(2,128)(2,1)} %param.23) | data formatting | bytes 13115392 | tf_op args[1]
  18.1 17.5 %copy.179 = bf16[2,1,1601,4,256]{4,0,2,1,3:T(2,128)(2,1)} copy(bf16[2,1,1601,4,256]{2,4,3,0,1:T(8,128)(2,1)} %bitcast.272) | data formatting | bytes 13115392 | tf_op jit(solution)/shard_map/reshape | solution.py:176
  35.6 147.6 %all_to_all.33 = bf16[2,1,1601,4,256]{4,0,2,1,3:T(2,128)(2,1)S(1)} all-to-all(bf16[2,1,1601,4,256]{4,0,2,1,3:T(2,128)(2,1)} %copy.179), channel_id=1, replica_groups=mesh['seq'=8,'enc'=4] {'enc'}, dimensions={3} | all-to-all | bytes 13115392 | tf_op jit(solution)/shard_map/all_to_all | solution.py:177
  183.2 10.8 %copy.222 = bf16[2,1,1601,4,256]{4,3,2,0,1:T(4,128)(2,1)} copy(bf16[2,1,1601,4,256]{4,0,2,1,3:T(2,128)(2,1)S(1)} %all_to_all.33) | data formatting | bytes 13115392 | tf_op jit(solution)/shard_map/all_to_all | solution.py:177
  201.3 68.5 %collective-permute-done = bf16[2,4,1601,1,256]{4,1,3,2,0:T(4,128)(2,1)} collective-permute-done((bf16[2,4,1601,1,256]{4,1,3,2,0:T(4,128)(2,1)}, bf16[2,4,1601,1,256]{4,1,3,2,0:T(4,128)(2,1)}, u32[]{:S(2)}, u32[]{:S(2)}) %collective-permute-start) | collective-permute-done | bytes 6557728 | tf_op jit(solution)/shard_map/ppermute | solution.py:16
  287.9 57.0 %while.66 = (s32[]{:T(128)}, f32[128,8]{0,1:T(8,128)S(1)}, f32[128,8]{0,1:T(8,128)S(1)}, f32[128,8,128]{2,0,1:T(8,128)S(1)}, pred[8]{0:T(512)(128)(4,1)S(1)}, /*...) while((s32[]{:T(128)}, f32[128,8]{0,1:T(8,128)S(1)}, ...), condition=%wide.region_9.10_spmd.clone, body=%wide.region_4.9_spmd.clone.sunk | while | flops 857687040 | bytes 21876196 | solution.py:88
  351.5 68.4 %while.67 = (s32[]{:T(128)}, f32[128,8]{0,1:T(8,128)S(1)}, f32[128,8]{0,1:T(8,128)S(1)}, f32[128,8,128]{2,0,1:T(8,128)S(1)}, pred[8]{0:T(512)(128)(4,1)S(1)}, /*...) while((s32[]{:T(128)}, f32[128,8]{0,1:T(8,128)S(1)}, ...), condition=%wide.region_15.16_spmd.clone, body=%wide.region_10.15_spmd.clone.sunk | while | flops 857687040 | bytes 21876196 | solution.py:88
  425.8 86.1 %while.68 = (s32[]{:T(128)}, f32[128,8,128]{2,0,1:T(8,128)S(1)}, bf16[8,1601,128]{2,1,0:T(8,128)(2,1)}, bf16[8,1601,128]{2,1,0:T(8,128)(2,1)}, pred[8]{0:T(512)(...) while((s32[]{:T(128)}, f32[128,8,128]{2,0,1:T(8,128)S(1)}, ...), condition=%wide.region_20.21_spmd.clone, body=%wide.region_17.20_spmd.clone.sunk | while | flops 2115737984 | bytes 35321188 | solution.py:156
  427.0 9.7 %conditional.14 = (f32[128,8,128]{2,0,1:T(8,128)S(1)}, bf16[1,1601,128]{2,1,0:T(8,128)(2,1)S(1)}, bf16[1,1601,128]{2,1,0:T(8,128)(2,1)S(1)}) conditional(s32[]{:T(128)} %bitcast.269, f32[128,8,128]{2,0,1:T(8,128)S(1)} %get-tuple-element.1876, (pred[8]{0:T(512)(128)(4,1)S(1)}, s32[]{:T(128)}, bf16[8,1601,128]{2,1,0:T(8,128)(2,1)}, ...), branch_computations={%region_18.18_spmd, %region_19.19_spmd.clone} | conditional | flops 2115737984 | bytes 33677412 | solution.py:154
  439.0 9.7 %conditional.14 = (f32[128,8,128]{2,0,1:T(8,128)S(1)}, bf16[1,1601,128]{2,1,0:T(8,128)(2,1)S(1)}, bf16[1,1601,128]{2,1,0:T(8,128)(2,1)S(1)}) conditional(s32[]{:T(128)} %bitcast.269, f32[128,8,128]{2,0,1:T(8,128)S(1)} %get-tuple-element.1876, (pred[8]{0:T(512)(128)(4,1)S(1)}, s32[]{:T(128)}, bf16[8,1601,128]{2,1,0:T(8,128)(2,1)}, ...), branch_computations={%region_18.18_spmd, %region_19.19_spmd.clone} | conditional | flops 2115737984 | bytes 33677412 | solution.py:154
  450.9 9.7 %conditional.14 = (f32[128,8,128]{2,0,1:T(8,128)S(1)}, bf16[1,1601,128]{2,1,0:T(8,128)(2,1)S(1)}, bf16[1,1601,128]{2,1,0:T(8,128)(2,1)S(1)}) conditional(s32[]{:T(128)} %bitcast.269, f32[128,8,128]{2,0,1:T(8,128)S(1)} %get-tuple-element.1876, (pred[8]{0:T(512)(128)(4,1)S(1)}, s32[]{:T(128)}, bf16[8,1601,128]{2,1,0:T(8,128)(2,1)}, ...), branch_computations={%region_18.18_spmd, %region_19.19_spmd.clone} | conditional | flops 2115737984 | bytes 33677412 | solution.py:154
  465.2 9.7 %conditional.14 = (f32[128,8,128]{2,0,1:T(8,128)S(1)}, bf16[1,1601,128]{2,1,0:T(8,128)(2,1)S(1)}, bf16[1,1601,128]{2,1,0:T(8,128)(2,1)S(1)}) conditional(s32[]{:T(128)} %bitcast.269, f32[128,8,128]{2,0,1:T(8,128)S(1)} %get-tuple-element.1876, (pred[8]{0:T(512)(128)(4,1)S(1)}, s32[]{:T(128)}, bf16[8,1601,128]{2,1,0:T(8,128)(2,1)}, ...), branch_computations={%region_18.18_spmd, %region_19.19_spmd.clone} | conditional | flops 2115737984 | bytes 33677412 | solution.py:154
  477.2 9.7 %conditional.14 = (f32[128,8,128]{2,0,1:T(8,128)S(1)}, bf16[1,1601,128]{2,1,0:T(8,128)(2,1)S(1)}, bf16[1,1601,128]{2,1,0:T(8,128)(2,1)S(1)}) conditional(s32[]{:T(128)} %bitcast.269, f32[128,8,128]{2,0,1:T(8,128)S(1)} %get-tuple-element.1876, (pred[8]{0:T(512)(128)(4,1)S(1)}, s32[]{:T(128)}, bf16[8,1601,128]{2,1,0:T(8,128)(2,1)}, ...), branch_computations={%region_18.18_spmd, %region_19.19_spmd.clone} | conditional | flops 2115737984 | bytes 33677412 | solution.py:154
  489.2 9.7 %conditional.14 = (f32[128,8,128]{2,0,1:T(8,128)S(1)}, bf16[1,1601,128]{2,1,0:T(8,128)(2,1)S(1)}, bf16[1,1601,128]{2,1,0:T(8,128)(2,1)S(1)}) conditional(s32[]{:T(128)} %bitcast.269, f32[128,8,128]{2,0,1:T(8,128)S(1)} %get-tuple-element.1876, (pred[8]{0:T(512)(128)(4,1)S(1)}, s32[]{:T(128)}, bf16[8,1601,128]{2,1,0:T(8,128)(2,1)}, ...), branch_computations={%region_18.18_spmd, %region_19.19_spmd.clone} | conditional | flops 2115737984 | bytes 33677412 | solution.py:154
  501.1 9.7 %conditional.14 = (f32[128,8,128]{2,0,1:T(8,128)S(1)}, bf16[1,1601,128]{2,1,0:T(8,128)(2,1)S(1)}, bf16[1,1601,128]{2,1,0:T(8,128)(2,1)S(1)}) conditional(s32[]{:T(128)} %bitcast.269, f32[128,8,128]{2,0,1:T(8,128)S(1)} %get-tuple-element.1876, (pred[8]{0:T(512)(128)(4,1)S(1)}, s32[]{:T(128)}, bf16[8,1601,128]{2,1,0:T(8,128)(2,1)}, ...), branch_computations={%region_18.18_spmd, %region_19.19_spmd.clone} | conditional | flops 2115737984 | bytes 33677412 | solution.py:154
  524.1 85.9 %while.69 = (s32[]{:T(128)}, f32[128,8,128]{2,0,1:T(8,128)S(1)}, bf16[8,1601,128]{2,1,0:T(8,128)(2,1)}, bf16[8,1601,128]{2,1,0:T(8,128)(2,1)}, pred[8]{0:T(512)(...) while((s32[]{:T(128)}, f32[128,8,128]{2,0,1:T(8,128)S(1)}, ...), condition=%wide.region_24.25_spmd.clone, body=%wide.region_21.24_spmd.clone.sunk | while | flops 2115737984 | bytes 35321188 | solution.py:156
  525.8 9.7 %conditional.15 = (f32[128,8,128]{2,0,1:T(8,128)S(1)}, bf16[1,1601,128]{2,1,0:T(8,128)(2,1)S(1)}, bf16[1,1601,128]{2,1,0:T(8,128)(2,1)S(1)}) conditional(s32[]{:T(128)} %bitcast.270, f32[128,8,128]{2,0,1:T(8,128)S(1)} %get-tuple-element.1828, (pred[8]{0:T(512)(128)(4,1)S(1)}, s32[]{:T(128)}, bf16[8,1601,128]{2,1,0:T(8,128)(2,1)}, ...), branch_computations={%region_22.22_spmd, %region_23.23_spmd.clone} | conditional | flops 2115737984 | bytes 33677412 | solution.py:154
  537.6 9.7 %conditional.15 = (f32[128,8,128]{2,0,1:T(8,128)S(1)}, bf16[1,1601,128]{2,1,0:T(8,128)(2,1)S(1)}, bf16[1,1601,128]{2,1,0:T(8,128)(2,1)S(1)}) conditional(s32[]{:T(128)} %bitcast.270, f32[128,8,128]{2,0,1:T(8,128)S(1)} %get-tuple-element.1828, (pred[8]{0:T(512)(128)(4,1)S(1)}, s32[]{:T(128)}, bf16[8,1601,128]{2,1,0:T(8,128)(2,1)}, ...), branch_computations={%region_22.22_spmd, %region_23.23_spmd.clone} | conditional | flops 2115737984 | bytes 33677412 | solution.py:154
  563.8 9.7 %conditional.15 = (f32[128,8,128]{2,0,1:T(8,128)S(1)}, bf16[1,1601,128]{2,1,0:T(8,128)(2,1)S(1)}, bf16[1,1601,128]{2,1,0:T(8,128)(2,1)S(1)}) conditional(s32[]{:T(128)} %bitcast.270, f32[128,8,128]{2,0,1:T(8,128)S(1)} %get-tuple-element.1828, (pred[8]{0:T(512)(128)(4,1)S(1)}, s32[]{:T(128)}, bf16[8,1601,128]{2,1,0:T(8,128)(2,1)}, ...), branch_computations={%region_22.22_spmd, %region_23.23_spmd.clone} | conditional | flops 2115737984 | bytes 33677412 | solution.py:154
  635.3 74.1 %collective-permute-done.1 = bf16[2,4,1601,1,256]{4,1,3,2,0:T(4,128)(2,1)S(1)} collective-permute-done((bf16[2,4,1601,1,256]{4,1,3,2,0:T(4,128)(2,1)S(1)}, bf16[2,4,1601,1,256]{4,1,3,2,0:T(4,128)(2,1)S(1)}, u32[]{:S(2)}, u32[]{:S(2)}) %collective-permute-start.1) | collective-permute-done | bytes 6557728 | tf_op jit(solution)/shard_map/ppermute | solution.py:16
  715.1 20.6 %copy.208 = bf16[2,4,1601,1,256]{4,0,3,2,1:T(2,128)(2,1)} copy(bf16[2,4,1601,1,256]{4,1,3,2,0:T(4,128)(2,1)S(1)} %add_convert_fusion) | data formatting | bytes 13115392 | tf_op jit(solution)/shard_map/convert_element_type | solution.py:215
  743.6 78.5 %all-to-all-done.1 = bf16[2,4,1601,1,256]{4,0,3,2,1:T(2,128)(2,1)} async-done(((bf16[2,4,1601,1,256]{4,0,3,2,1:T(2,128)(2,1)}), bf16[2,4,1601,1,256]{4,0,3,2,1:T(2,128)(2,1)}, u32[]{:S(2)}, u32[]{:S(2)}) %all-to-all-start.1) | async-done | bytes 6557728 | tf_op jit(solution)/shard_map/all_to_all | solution.py:218
  822.2 17.3 %copy.213 = bf16[2,4,1601,1,256]{2,4,1,0,3:T(8,128)(2,1)} copy(bf16[2,4,1601,1,256]{4,0,3,2,1:T(2,128)(2,1)} %all-to-all-done.1) | data formatting | bytes 13115392 | tf_op jit(solution)/shard_map/all_to_all | solution.py:218
  839.4 17.5 %copy.212 = bf16[2,1,1601,1024]{3,0,2,1:T(2,128)(2,1)} copy(bf16[2,1,1601,1024]{2,3,0,1:T(8,128)(2,1)} %bitcast.271) | data formatting | bytes 13115392
  (361 shorter events, 484.1 us)
Async XLA Ops:
  183.2 16.0 %copy-start.5 = (bf16[128,2048]{1,0:T(8,128)(2,1)S(1)}, bf16[128,2048]{1,0:T(8,128)(2,1)}, u32[]{:S(2)}) copy-start(bf16[128,2048]{1,0:T(8,128)(2,1)} %param.22) | copy-start | bytes 1572868
  183.2 16.7 %copy-start.6 = (bf16[128,2048]{1,0:T(8,128)(2,1)S(1)}, bf16[128,2048]{1,0:T(8,128)(2,1)}, u32[]{:S(2)}) copy-start(bf16[128,2048]{1,0:T(8,128)(2,1)} %param.27) | copy-start | bytes 1572868
  183.2 17.7 %copy-start.7 = (s32[8,2]{0,1:T(2,128)S(1)}, s32[8,2]{0,1:T(2,128)}, u32[]{:S(2)}) copy-start(s32[8,2]{0,1:T(2,128)} %param.24) | copy-start | bytes 196
  183.2 17.7 %copy-start.8 = (s32[8]{0:T(128)S(1)}, s32[8]{0:T(128)}, u32[]{:S(2)}) copy-start(s32[8]{0:T(128)} %param.25) | copy-start | bytes 100
  194.0 75.9 %collective-permute-start = (bf16[2,4,1601,1,256]{4,1,3,2,0:T(4,128)(2,1)}, bf16[2,4,1601,1,256]{4,1,3,2,0:T(4,128)(2,1)}, u32[]{:S(2)}, u32[]{:S(2)}) collective-permute-start(bf16[2,4,1601,1,256]{4,1,3,2,0:T(4,128)(2,1)} %bitcast.257), channel_id=1, source_target_pairs={{0,4},{4,8},{8,12},{12,16},{16,20},{20,24},{24,28},{1,5},{5,9},{9,... | collective-permute-start | bytes 19673096 | tf_op jit(solution)/shard_map/ppermute | solution.py:16
  345.1 4.2 copy-start.3
  610.0 6.7 copy-start.1
  610.0 12.9 %copy-start = (bf16[8,1601,128]{2,1,0:T(8,128)(2,1)S(1)}, bf16[8,1601,128]{2,1,0:T(8,128)(2,1)}, u32[]{:S(2)}) copy-start(bf16[8,1601,128]{2,1,0:T(8,128)(2,1)} %get-tuple-element.576) | copy-start | bytes 9836548
  616.7 12.1 %copy-start.2 = (bf16[8,1601,128]{2,0,1:T(8,128)(2,1)S(1)}, bf16[8,1601,128]{2,0,1:T(8,128)(2,1)}, u32[]{:S(2)}) copy-start(bf16[8,1601,128]{2,0,1:T(8,128)(2,1)} %copy.226) | copy-start | bytes 9836548
  633.4 76.0 %collective-permute-start.1 = (bf16[2,4,1601,1,256]{4,1,3,2,0:T(4,128)(2,1)S(1)}, bf16[2,4,1601,1,256]{4,1,3,2,0:T(4,128)(2,1)S(1)}, u32[]{:S(2)}, u32[]{:S(2)}) collective-permute-start(bf16[2,4,1601,1,256]{4,1,3,2,0:T(4,128)(2,1)S(1)} %pad_maximum_fusion), channel_id=1, source_target_pairs={{4,0},{8,4},{12,8},{16,12},{20,16},{24,20},{28,24},{5,1},{9,5},{13... | collective-permute-start | bytes 19673096 | tf_op jit(solution)/shard_map/ppermute | solution.py:16
  735.7 6.9 copy-start.4
  735.7 86.5 %all-to-all-start.1 = ((bf16[2,4,1601,1,256]{4,0,3,2,1:T(2,128)(2,1)}), bf16[2,4,1601,1,256]{4,0,3,2,1:T(2,128)(2,1)}, u32[]{:S(2)}, u32[]{:S(2)}) async-start(bf16[2,4,1601,1,256]{4,0,3,2,1:T(2,128)(2,1)} %copy.208), calls=%async_computation.1 | async-start | bytes 13115392 | tf_op jit(solution)/shard_map/all_to_all | solution.py:218
where the time goes:
time: 841 us; the launch traced here: 857 us
  waiting for transfers between devices  221 us (26%)
  matrix products  208 us (25%)
  local copies, waits for them, and re-layouts  190 us (23%)
  blocking collectives  148 us (18%)
  other arithmetic  41.4 us (5%)
  loops' own time  34.4 us (4%)
  starting transfers between devices  12.6 us (1%)
    all_to_all x1, blocking collectives, shards(): lax.all_to_all(split_kv, 'enc', split_axis=3, concat_axis=1, tiled=True)  148 us
    ppermute x2, waiting for transfers between devices, shifted(): return lax.ppermute(shard, axis, pairs)  143 us
    all_to_all x1, waiting for transfers between devices, shards(): lax.all_to_all(row_grads, 'enc', split_axis=1, concat_axis=3, tiled=True)  78.5 us
    dot_general x28, matrix products, score_block(): jnp.einsum('tgd,jd->tgj', query_head, key_tile, preferred_element_type=jn...  57.6 us
    unnamed x32, local copies, waits for them, and re-layouts  48.9 us
    dot_general x14, matrix products, online_update(): jnp.einsum('tgj,jd->tgd', probs.astype(jnp.bfloat16), value_tile, preferr...  44.7 us
    dot_general x14, matrix products, grad_update(): jnp.einsum('tgd,jd->tgj', grad_head, value_tile, preferred_element_type=j...  41.6 us
    dot_general x14, matrix products, grad_update(): jnp.einsum('tgj,jd->tgd', grad_scores, key_tile, preferred_element_type=j...  30.1 us
  transfers between devices with their start and end apart: 3, of which 3 were waited for; matrix products, arithmetic and copies ran while one was open for 0% of the time, Pallas kernels for 0%

commit v1 on v0

v1 whole, which is shorter than its diff:
```python
import functools

import jax
import jax.numpy as jnp
from jax import lax
from jax.experimental import pallas as pl
from jax.experimental.pallas import tpu as pltpu
from jax.sharding import PartitionSpec as P

HEAD_SIZE = 128
TILES = 4
LOW = -1e30
HIGH = 1e30
SCALE = HEAD_SIZE ** (-0.5)
LOG2E = 1.4426950408889634
BLOCK = 512
ROW_PAD = 16


def rotated(x, axis, by):
    total = lax.axis_size(axis)
    return lax.ppermute(x, axis, [(i, (i + by) % total) for i in range(total)])


def shifted(x, axis, by):
    total = lax.axis_size(axis)
    return lax.ppermute(x, axis, [(i, i + by) for i in range(total) if 0 <= i + by < total])


def dot_nt(a, b):
    return lax.dot_general(a, b, (((1,), (1,)), ((), ())), preferred_element_type=jnp.float32)


def dot_tn(a, b):
    return lax.dot_general(a, b, (((0,), (0,)), ((), ())), preferred_element_type=jnp.float32)


def dot_nn(a, b):
    return lax.dot_general(a, b, (((1,), (0,)), ((), ())), preferred_element_type=jnp.float32)


def stacked(ref, groups):
    return jnp.concatenate(
        [ref[0, :, i * HEAD_SIZE : (i + 1) * HEAD_SIZE] for i in range(groups)], axis=0
    )


def cuts(tokens, padded):
    whole = tokens // BLOCK
    parts = [(i * BLOCK, BLOCK, BLOCK) for i in range(whole)]
    if padded > whole * BLOCK:
        parts.append((whole * BLOCK, padded - whole * BLOCK, tokens - whole * BLOCK))
    return parts


def row_fill(values, valid, fill):
    if values.shape[0] == valid:
        return values
    rows = lax.broadcasted_iota(jnp.int32, values.shape, 0)
    return jnp.where(rows < valid, values, fill)


def forward_kernel(tokens, groups, at_ref, q_ref, g_ref, k_ref, v_ref, o_ref, lse_ref, delta_ref, s_ref):
    padded = k_ref.shape[2]
    parts = cuts(tokens, padded)
    q = stacked(q_ref, groups)
    top = None
    for start, size, valid in parts:
        s = dot_nt(k_ref[0, 0, start : start + size], q)
        s = row_fill(s, valid, LOW)
        s_ref[start : start + size] = s
        peak = jnp.max(s, axis=0, keepdims=True)
        top = peak if top is None else jnp.maximum(top, peak)
    top = top * (SCALE * LOG2E)
    total = None
    out = None
    for start, size, valid in parts:
        p = jnp.exp2(s_ref[start : start + size] * (SCALE * LOG2E) - top)
        part_total = jnp.sum(p, axis=0, keepdims=True)
        part_out = dot_tn(v_ref[0, 0, start : start + size], p.astype(jnp.bfloat16))
        total = part_total if total is None else total + part_total
        out = part_out if out is None else out + part_out
    out = out / total
    lse = top + jnp.log2(total)
    o_ref[0] = out
    for i in range(groups):
        span = slice(i * HEAD_SIZE, (i + 1) * HEAD_SIZE)
        g_t = g_ref[0, :, span].astype(jnp.float32).T
        lse_ref[0, i : i + 1] = lse[:, span]
        delta_ref[0, i : i + 1] = jnp.sum(g_t * out[:, span], axis=0, keepdims=True)


def backward_kernel(
    tokens,
    groups,
    first,
    at_ref,
    q_ref,
    g_ref,
    k_ref,
    v_ref,
    o_ref,
    lse_ref,
    delta_ref,
    weight_ref,
    *rest,
):
    if first:
        old_ref, mix_ref, dq_ref, dkv_ref = rest
        mix_in_ref = dq_in_ref = None
    else:
        mix_in_ref, dq_in_ref, old_ref, mix_ref, dq_ref, dkv_ref = rest
    padded = k_ref.shape[2]
    q = stacked(q_ref, groups)
    g = stacked(g_ref, groups)
    lse = jnp.concatenate([lse_ref[0, i : i + 1] for i in range(groups)], axis=1)
    delta = jnp.concatenate([delta_ref[0, i : i + 1] for i in range(groups)], axis=1)
    grad_q = None
    for start, size, valid in cuts(tokens, padded):
        k = k_ref[0, 0, start : start + size]
        v = v_ref[0, 0, start : start + size]
        w = jnp.exp2(dot_nt(k, q) * (SCALE * LOG2E) - lse)
        w = row_fill(w, valid, 0.0)
        ds = (w * (dot_nt(v, g) - delta)).astype(jnp.bfloat16)
        dv = dot_nn(w.astype(jnp.bfloat16), g)
        dk = dot_nn(ds, q) * SCALE
        dkv_ref[0, 0, start : start + valid] = dk[:valid].astype(jnp.bfloat16)
        dkv_ref[1, 0, start : start + valid] = dv[:valid].astype(jnp.bfloat16)
        part = dot_tn(k, ds)
        grad_q = part if grad_q is None else grad_q + part
    for i in range(groups):
        span = slice(i * HEAD_SIZE, (i + 1) * HEAD_SIZE)
        mix = (o_ref[0, :, span] * weight_ref[0, i : i + 1]).T
        dq = (grad_q[:, span] * SCALE).T
        if not first:
            mix = mix + mix_in_ref[:, span].astype(jnp.float32)
            dq = dq + dq_in_ref[:, span].astype(jnp.float32)
        mix_ref[:, span] = mix.astype(jnp.bfloat16)
        dq_ref[:, span] = dq.astype(jnp.bfloat16)


def forward_call(at, rows, image_kv, tokens, groups, heads):
    text = rows.shape[1]
    width = groups * HEAD_SIZE
    padded = image_kv.shape[2]
    lanes = groups * text
    stat = jax.ShapeDtypeStruct((heads, groups, text), jnp.float32)
    return pl.pallas_call(
        functools.partial(forward_kernel, tokens, groups),
        grid_spec=pltpu.PrefetchScalarGridSpec(
            num_scalar_prefetch=1,
            grid=(heads,),
            in_specs=[
                pl.BlockSpec((1, text, width), lambda h, at: (at[1], 0, h)),
                pl.BlockSpec((1, text, width), lambda h, at: (at[1], 0, heads + h)),
                pl.BlockSpec((1, 1, padded, HEAD_SIZE), lambda h, at: (0, 0, 0, at[0] * heads + h)),
                pl.BlockSpec((1, 1, padded, HEAD_SIZE), lambda h, at: (1, 0, 0, at[0] * heads + h)),
            ],
            out_specs=[
                pl.BlockSpec((1, HEAD_SIZE, lanes), lambda h, at: (h, 0, 0)),
                pl.BlockSpec((1, groups, text), lambda h, at: (h, 0, 0)),
                pl.BlockSpec((1, groups, text), lambda h, at: (h, 0, 0)),
            ],
            scratch_shapes=[pltpu.VMEM((padded, lanes), jnp.float32)],
        ),
        out_shape=[jax.ShapeDtypeStruct((heads, HEAD_SIZE, lanes), jnp.float32), stat, stat],
        compiler_params=pltpu.CompilerParams(vmem_limit_bytes=48 * 1024 * 1024),
        cost_estimate=pl.CostEstimate(
            flops=heads * 8 * padded * lanes * HEAD_SIZE,
            bytes_accessed=heads * padded * HEAD_SIZE * 4,
            transcendentals=heads * padded * lanes,
        ),
        name="forward_group",
    )(at, rows, rows, image_kv, image_kv)


def backward_call(at, rows, image_kv, mixed, lse, delta, weight, carried, grads, tokens, groups, heads):
    text = rows.shape[1]
    width = groups * HEAD_SIZE
    padded = image_kv.shape[2]
    lanes = groups * text
    first = carried is None
    stat = pl.BlockSpec((1, groups, text), lambda h, at: (h, 0, 0))
    part = pl.BlockSpec((text, width), lambda h, at: (0, h))
    in_specs = [
        pl.BlockSpec((1, text, width), lambda h, at: (at[1], 0, h)),
        pl.BlockSpec((1, text, width), lambda h, at: (at[1], 0, heads + h)),
        pl.BlockSpec((1, 1, padded, HEAD_SIZE), lambda h, at: (0, 0, 0, at[0] * heads + h)),
        pl.BlockSpec((1, 1, padded, HEAD_SIZE), lambda h, at: (1, 0, 0, at[0] * heads + h)),
        pl.BlockSpec((1, HEAD_SIZE, lanes), lambda h, at: (h, 0, 0)),
        stat,
        stat,
        stat,
    ]
    operands = [at, rows, rows, image_kv, image_kv, mixed, lse, delta, weight]
    if not first:
        in_specs += [part, pl.BlockSpec((text, width), lambda h, at: (0, heads + h))]
        operands += [carried, carried]
    aliases = {}
    in_specs.append(pl.BlockSpec(memory_space=pl.ANY))
    operands.append(grads)
    aliases = {len(operands) - 1: 2}
    grad_shape = grads.shape
    out = jax.ShapeDtypeStruct((text, heads * width), jnp.bfloat16)
    mix, dq, grads = pl.pallas_call(
        functools.partial(backward_kernel, tokens, groups, first),
        grid_spec=pltpu.PrefetchScalarGridSpec(
            num_scalar_prefetch=1,
            grid=(heads,),
            in_specs=in_specs,
            out_specs=[
                part,
                part,
                pl.BlockSpec((2, 1, tokens, HEAD_SIZE), lambda h, at: (0, 0, 0, at[0] * heads + h)),
            ],
        ),
        out_shape=[out, out, jax.ShapeDtypeStruct(grad_shape, jnp.bfloat16)],
        input_output_aliases=aliases,
        compiler_params=pltpu.CompilerParams(vmem_limit_bytes=48 * 1024 * 1024),
        cost_estimate=pl.CostEstimate(
            flops=heads * 20 * padded * lanes * HEAD_SIZE,
            bytes_accessed=heads * padded * HEAD_SIZE * 8,
            transcendentals=heads * padded * lanes,
        ),
        name="backward_group",
    )(*operands)
    return jnp.concatenate([mix, dq], axis=1), grads


def joined(first_lse, first_delta, second_lse, second_delta):
    top = jnp.maximum(first_lse, second_lse)
    first = jnp.exp2(first_lse - top)
    second = jnp.exp2(second_lse - top)
    total = first + second
    return top + jnp.log2(total), (first * first_delta + second * second_delta) / total


def shards(queries, image_key_value, image_spans, tile_counts, cross_gate, grad_out):
    seq_index = lax.axis_index("seq")
    enc_index = lax.axis_index("enc")
    enc_total = lax.axis_size("enc")
    text = queries.shape[0]
    tokens = image_key_value.shape[2]
    heads = image_key_value.shape[3] // (enc_total * HEAD_SIZE)
    groups = queries.shape[1] // (heads * HEAD_SIZE)
    row_images = enc_total // TILES
    gate = jnp.tanh(cross_gate[0])
    grad_mixed = (gate * grad_out.astype(jnp.float32)).astype(jnp.bfloat16)

    own = jnp.concatenate([queries, grad_mixed], axis=1)
    later = shifted(own, "seq", -1)
    spans = lax.dynamic_slice_in_dim(image_spans, seq_index * row_images, row_images, 0)
    offsets = spans[:, 0] - seq_index * text
    slots = jnp.arange(text, dtype=jnp.int32)
    in_own = slots[None, :] >= offsets[:, None]
    positions = jnp.where(in_own, seq_index * text, (seq_index + 1) * text) + slots[None, :]
    seen = (positions >= spans[:, :1]) & (positions < spans[:, 1:])
    window = jnp.where(in_own[:, :, None], own[None], later[None])

    padding = (-tokens) % ROW_PAD
    image_kv = jnp.pad(image_key_value, ((0, 0), (0, 0), (0, padding), (0, 0)))

    place = enc_index // TILES
    image = seq_index * row_images + place
    in_use = (enc_index - place * TILES) < lax.dynamic_index_in_dim(tile_counts, image, 0, False)
    my_seen = lax.dynamic_index_in_dim(seen, place, 0, False) & in_use
    my_own = lax.dynamic_index_in_dim(in_own, place, 0, False)

    rings = [window]
    for step in range(1, enc_total):
        rings.append(rotated(rings[-1], "enc", 1))
    places = []
    results = []
    for step in range(enc_total):
        source = lax.rem(enc_index - step + enc_total, enc_total)
        at = jnp.stack([source, place]).astype(jnp.int32)
        places.append(at)
        results.append(forward_call(at, rings[step], image_kv, tokens, groups, heads))

    lse_ring = jnp.stack([r[1] for r in results])
    delta_ring = jnp.stack([r[2] for r in results])
    lse_ring = jnp.where(my_seen, lse_ring, LOW)
    delta_ring = jnp.where(my_seen, delta_ring, 0.0)
    order = lax.rem(enc_index - jnp.arange(enc_total) + enc_total, enc_total)
    lse_all = jnp.take(lse_ring, order, axis=0)
    delta_all = jnp.take(delta_ring, order, axis=0)
    gathered = lax.all_gather(jnp.stack([lse_all, delta_all]), "enc")
    upper = None
    lower = None
    for tile in range(enc_total):
        mine = in_own[tile // TILES]
        lse_tile, delta_tile = gathered[tile, 0], gathered[tile, 1]
        up = (jnp.where(mine, lse_tile, LOW), delta_tile)
        down = (jnp.where(mine, LOW, lse_tile), delta_tile)
        upper = up if upper is None else joined(*upper, *up)
        lower = down if lower is None else joined(*lower, *down)
    edge = jnp.arange(lax.axis_size("seq"))
    before = shifted(jnp.stack(lower), "seq", 1)
    after = shifted(jnp.stack(upper), "seq", -1)
    before_lse = jnp.where(seq_index > 0, before[0], LOW)
    after_lse = jnp.where(seq_index < lax.axis_size("seq") - 1, after[0], LOW)
    own_total = joined(*upper, before_lse, before[1])
    next_total = joined(*lower, after_lse, after[1])
    full_lse = jnp.where(my_own, own_total[0], next_total[0])
    full_delta = jnp.where(my_own, own_total[1], next_total[1])
    weight_all = jnp.where(my_seen, jnp.exp2(lse_all - full_lse), 0.0) * gate
    full_lse = jnp.where(my_seen, full_lse, HIGH)

    grads = jnp.zeros(image_key_value.shape, jnp.bfloat16)
    carried = None
    for step in list(range(1, enc_total)) + [0]:
        source = places[step][0]
        if carried is not None:
            carried = rotated(carried, "enc", 1)
        pick = lambda a: lax.dynamic_index_in_dim(a, source, 0, False)
        accumulated = carried
        if row_images > 1 and carried is not None:
            accumulated = lax.dynamic_index_in_dim(carried, place, 0, False)
        message, grads = backward_call(
            places[step],
            rings[step],
            image_kv,
            results[step][0],
            pick(full_lse),
            pick(full_delta),
            pick(weight_all),
            accumulated,
            grads,
            tokens,
            groups,
            heads,
        )
        if row_images > 1:
            base = jnp.zeros((row_images,) + message.shape, message.dtype) if carried is None else carried
            message = lax.dynamic_update_index_in_dim(base, message, place, 0)
        carried = message

    sums = carried.reshape(row_images, text, -1).astype(jnp.float32)
    kept = jnp.sum(jnp.where(in_own[:, :, None], sums, 0.0), axis=0)
    passed = jnp.sum(jnp.where(in_own[:, :, None], 0.0, sums), axis=0).astype(jnp.bfloat16)
    total = (kept + shifted(passed, "seq", 1).astype(jnp.float32)).astype(jnp.bfloat16)
    width = queries.shape[1]
    return (total[:, :width], total[:, width:], grads)


def solution(mesh):
    in_specs = (
        P("seq", "enc"),
        P(None, ("seq", "enc"), None, None),
        P(),
        P(),
        P(),
        P("seq", "enc"),
    )
    out_specs = (P("seq", "enc"), P("seq", "enc"), P(None, ("seq", "enc"), None, None))
    return jax.shard_map(shards, mesh=mesh, in_specs=in_specs, out_specs=out_specs, check_vma=False)
```

time: 841 us -> 323 us (0.38)
  the two profiles are of different devices: /device:TPU:3 before, /device:TPU:1 now
where the time goes in v1:
time: 323 us; the launch traced here: 320 us
  waiting for transfers between devices  86.5 us (27%)
  Pallas kernels  75.3 us (23%)
  local copies, waits for them, and re-layouts  73.2 us (23%)
  starting transfers between devices  61.4 us (19%)
  blocking collectives  11.1 us (3%)
  other arithmetic  8.73 us (3%)
  between operations  3.35 us (1%)
    ppermute x6, waiting for transfers between devices, rotated(): return lax.ppermute(x, axis, [(i, (i + by) % total) for i in range(total)])  71.1 us
    unnamed x28, local copies, waits for them, and re-layouts  59.4 us
    ppermute x4, starting transfers between devices, shifted(): lax.ppermute(x, axis, [(i, i + by) for i in range(total) if 0 <= i + by <...  56.5 us
    pallas_call x4, Pallas kernels, backward_call(): pl.pallas_call(functools.partial(backward_kernel, tokens, groups, first),...  47 us
    pallas_call x4, Pallas kernels, forward_call(): pl.pallas_call(functools.partial(forward_kernel, tokens, groups), grid_sp...  28.3 us
    ppermute x4, waiting for transfers between devices, shifted(): lax.ppermute(x, axis, [(i, i + by) for i in range(total) if 0 <= i + by <...  15.4 us
    all_gather x1, blocking collectives, shards(): gathered = lax.all_gather(jnp.stack([lse_all, delta_all]), 'enc')  11.1 us
    pad x1, local copies, waits for them, and re-layouts, shards(): image_kv = jnp.pad(image_key_value, ((0, 0), (0, 0), (0, padding), (0, 0)))  6.66 us
  transfers between devices with their start and end apart: 10, of which 7 were waited for; matrix products, arithmetic and copies ran while one was open for 21% of the time, Pallas kernels for 7%

profile of v1, /device:TPU:1, one launch (start us, length us, event | category | flops | bytes accessed | tf_op | source)
XLA Modules:
  0.0 319.6 jit_solution(7157487202994853885)
XLA Ops:
  3.7 2.0 collective-permute-start
  6.9 14.0 %collective-permute-done = bf16[128,4096]{1,0:T(8,128)(2,1)S(1)} collective-permute-done((bf16[128,4096]{1,0:T(8,128)(2,1)S(1)}, bf16[128,4096]{1,0:T(8,128)(2,1)S(1)}, u32[]{:S(2)}, u32[]{:S(2)}) %collective-permute-start) | collective-permute-done | bytes 1048608 | tf_op jit(solution)/shard_map/ppermute | solution.py:27
  22.7 20.4 %collective-permute-done.1.q_ref.g_ref = bf16[1,128,4096]{2,1,0:T(8,128)(2,1)S(1)} collective-permute-done((bf16[1,128,4096]{2,1,0:T(8,128)(2,1)S(1)}, bf16[1,128,4096]{2,1,0:T(8,128)(2,1)S(1)}, u32[]{:S(2)}, u32[]{:S(2)}) %collective-permute-start.1) | collective-permute-done | bytes 1048608 | tf_op jit(solution)/shard_map/ppermute | solution.py:22
  44.3 7.8 %copy.17 = bf16[2,1,1601,1024]{3,2,1,0:T(8,128)(2,1)} copy(bf16[2,1,1601,1024]{3,0,2,1:T(2,128)(2,1)} %param.9) | data formatting | bytes 13115392 | tf_op args[1]
  53.4 6.7 %pad.4.k_ref.v_ref = bf16[2,1,1616,1024]{3,2,1,0:T(8,128)(2,1)} pad(bf16[2,1,1601,1024]{3,2,1,0:T(8,128)(2,1)} %copy.17, bf16[]{:T(256)} %constant.105.clone.1), padding=0_0x0_0x0_15x0_0 | pad | bytes 13176834 | tf_op jit(solution)/shard_map/jit(_pad)/pad | solution.py:261
  60.4 3.8 %collective-permute-done.2.q_ref.g_ref = bf16[1,128,4096]{2,1,0:T(8,128)(2,1)S(1)} collective-permute-done((bf16[1,128,4096]{2,1,0:T(8,128)(2,1)S(1)}, bf16[1,128,4096]{2,1,0:T(8,128)(2,1)S(1)}, u32[]{:S(2)}, u32[]{:S(2)}) %collective-permute-start.2) | collective-permute-done | bytes 1048608 | tf_op jit(solution)/shard_map/ppermute | solution.py:22
  64.2 1.7 collective-permute-start.3
  67.2 7.1 %forward_group.4 = (f32[2,128,1024]{2,1,0:T(8,128)S(1)}, f32[2,8,128]{2,1,0:T(8,128)S(1)}, f32[2,8,128]{2,1,0:T(8,128)S(1)}) custom-call(s32[2]{0:T(128)S(1)} %pad_add_fusion.at_ref, bf16[1,128,4096]{2,1,0:T(8,128)(2,1)S(1)} %select_bitcast_fusion.q_ref.g_ref, bf16[1,128,4096]{2,1,0:T(8,128)(2,1)S(1)} %select_bitcast_fusion.q_ref.g_ref, ...), custom_call_target="tpu_custom_call" | custom-call | flops 3388997632 | bytes 1654784 | tf_op jit(solution)/shard_map/forward_group/pallas_call | solution.py:148
  75.3 7.1 %forward_group.5 = (f32[2,128,1024]{2,1,0:T(8,128)S(1)}, f32[2,8,128]{2,1,0:T(8,128)S(1)}, f32[2,8,128]{2,1,0:T(8,128)S(1)}) custom-call(s32[2]{0:T(128)S(1)} %pad_add_fusion.1.at_ref, bf16[1,128,4096]{2,1,0:T(8,128)(2,1)S(1)} %collective-permute-done.1.q_ref.g_ref, bf16[1,128,4096]{2,1,0:T(8,128)(2,1)S(1)} %collective-permute-done.1.q_ref.g_ref, ...), custom_call_target="tpu_custom_call" | custom-call | flops 3388997632 | bytes 1654784 | tf_op jit(solution)/shard_map/forward_group/pallas_call | solution.py:148
  83.4 7.1 %forward_group.6 = (f32[2,128,1024]{2,1,0:T(8,128)S(1)}, f32[2,8,128]{2,1,0:T(8,128)S(1)}, f32[2,8,128]{2,1,0:T(8,128)S(1)}) custom-call(s32[2]{0:T(128)S(1)} %pad_add_fusion.2.at_ref, bf16[1,128,4096]{2,1,0:T(8,128)(2,1)S(1)} %collective-permute-done.2.q_ref.g_ref, bf16[1,128,4096]{2,1,0:T(8,128)(2,1)S(1)} %collective-permute-done.2.q_ref.g_ref, ...), custom_call_target="tpu_custom_call" | custom-call | flops 3388997632 | bytes 1654784 | tf_op jit(solution)/shard_map/forward_group/pallas_call | solution.py:148
  91.5 7.1 %forward_group.7 = (f32[2,128,1024]{2,1,0:T(8,128)S(1)}, f32[2,8,128]{2,1,0:T(8,128)S(1)}, f32[2,8,128]{2,1,0:T(8,128)S(1)}) custom-call(s32[2]{0:T(128)S(1)} %pad_add_fusion.3.at_ref, bf16[1,128,4096]{2,1,0:T(8,128)(2,1)S(1)} %collective-permute-done.3.q_ref.g_ref, bf16[1,128,4096]{2,1,0:T(8,128)(2,1)S(1)} %collective-permute-done.3.q_ref.g_ref, ...), custom_call_target="tpu_custom_call" | custom-call | flops 3388997632 | bytes 1654784 | tf_op jit(solution)/shard_map/forward_group/pallas_call | solution.py:148
  100.8 11.1 %all-gather = f32[8,4,2,8,128]{4,3,2,1,0:T(8,128)S(1)} all-gather(f32[2,4,2,8,128]{4,3,2,1,0:T(8,128)S(1)} %pad_maximum_fusion.5), channel_id=2, replica_groups=mesh['seq'=8,'enc'=4] {'enc'}, dimensions={0}, use_global_device_ids=true | all-gather | bytes 327680 | tf_op jit(solution)/shard_map/all_gather | solution.py:287
  112.8 1.9 collective-permute-start.5
  115.4 15.4 %collective-permute-start.4 = (f32[2,4,2,8,128]{4,3,2,1,0:T(8,128)}, f32[2,4,2,8,128]{4,3,2,1,0:T(8,128)}, u32[]{:S(2)}, u32[]{:S(2)}) collective-permute-start(f32[2,4,2,8,128]{4,3,2,1,0:T(8,128)} %pad_maximum_fusion.6), channel_id=1, source_target_pairs={{0,4},{4,8},{8,12},{12,16},{16,20},{20,24},{24,28},{1,5},{5,9},{9,... | collective-permute-start | bytes 196616 | tf_op jit(solution)/shard_map/ppermute | solution.py:27
  134.2 3.6 %broadcast_in_dim.112.clone.rest_0_ = bf16[2,1,1601,1024]{3,2,1,0:T(8,128)(2,1)} broadcast(bf16[]{:T(256)} %constant.105.clone.1), dimensions={} | broadcast | bytes 6557698 | tf_op jit(solution)/shard_map/broadcast_in_dim | solution.py:309
  137.8 11.6 %backward_group.4 = (bf16[128,2048]{1,0:T(8,128)(2,1)S(1)}, bf16[128,2048]{1,0:T(8,128)(2,1)S(1)}, bf16[2,1,1601,1024]{3,2,1,0:T(8,128)(2,1)}) custom-call(s32[2]{0:T(128)S(1)} %pad_add_fusion.1.at_ref, bf16[1,128,4096]{2,1,0:T(8,128)(2,1)S(1)} %collective-permute-done.1.q_ref.g_ref, ...), custom_call_target="tpu_custom_call", output_to_operand_aliasing={{2}: (9, {})} | custom-call | flops 8472494080 | bytes 3309568 | tf_op jit(solution)/shard_map/backward_group/pallas_call | solution.py:205
  149.7 15.2 %collective-permute-done.6.rest_0_.rest_1_ = bf16[128,4096]{1,0:T(8,128)(2,1)S(1)} collective-permute-done((bf16[128,4096]{1,0:T(8,128)(2,1)S(1)}, bf16[128,4096]{1,0:T(8,128)(2,1)S(1)}, u32[]{:S(2)}, u32[]{:S(2)}) %collective-permute-start.6) | collective-permute-done | bytes 1048608 | tf_op jit(solution)/shard_map/ppermute | solution.py:22
  165.0 11.8 %backward_group.5 = (bf16[128,2048]{1,0:T(8,128)(2,1)S(1)}, bf16[128,2048]{1,0:T(8,128)(2,1)S(1)}, bf16[2,1,1601,1024]{3,2,1,0:T(8,128)(2,1)}) custom-call(s32[2]{0:T(128)S(1)} %pad_add_fusion.2.at_ref, bf16[1,128,4096]{2,1,0:T(8,128)(2,1)S(1)} %collective-permute-done.2.q_ref.g_ref, ...), custom_call_target="tpu_custom_call", output_to_operand_aliasing={{2}: (11, {})} | custom-call | flops 8472494080 | bytes 3309568 | tf_op jit(solution)/shard_map/backward_group/pallas_call | solution.py:205
  177.1 15.4 %collective-permute-done.7.rest_0_.rest_1_ = bf16[128,4096]{1,0:T(8,128)(2,1)S(1)} collective-permute-done((bf16[128,4096]{1,0:T(8,128)(2,1)S(1)}, bf16[128,4096]{1,0:T(8,128)(2,1)S(1)}, u32[]{:S(2)}, u32[]{:S(2)}) %collective-permute-start.7) | collective-permute-done | bytes 1048608 | tf_op jit(solution)/shard_map/ppermute | solution.py:22
  192.6 11.8 %backward_group.6 = (bf16[128,2048]{1,0:T(8,128)(2,1)S(1)}, bf16[128,2048]{1,0:T(8,128)(2,1)S(1)}, bf16[2,1,1601,1024]{3,2,1,0:T(8,128)(2,1)}) custom-call(s32[2]{0:T(128)S(1)} %pad_add_fusion.3.at_ref, bf16[1,128,4096]{2,1,0:T(8,128)(2,1)S(1)} %copy-done.2, bf16[1,128,4096]{2,1,0:T(8,128)(2,1)S(1)} %copy-done.2, ...), custom_call_target="tpu_custom_call", output_to_operand_aliasing={{2}: (11, {})} | custom-call | flops 8472494080 | bytes 3309568 | tf_op jit(solution)/shard_map/backward_group/pallas_call | solution.py:205
  204.5 16.2 %collective-permute-done.8.rest_0_.rest_1_ = bf16[128,4096]{1,0:T(8,128)(2,1)S(1)} collective-permute-done((bf16[128,4096]{1,0:T(8,128)(2,1)S(1)}, bf16[128,4096]{1,0:T(8,128)(2,1)S(1)}, u32[]{:S(2)}, u32[]{:S(2)}) %collective-permute-start.8) | collective-permute-done | bytes 1048608 | tf_op jit(solution)/shard_map/ppermute | solution.py:22
  220.8 11.9 %backward_group.7 = (bf16[128,2048]{1,0:T(8,128)(2,1)S(1)}, bf16[128,2048]{1,0:T(8,128)(2,1)S(1)}, bf16[2,1,1601,1024]{3,2,1,0:T(8,128)(2,1)}) custom-call(s32[2]{0:T(128)S(1)} %pad_add_fusion.at_ref, bf16[1,128,4096]{2,1,0:T(8,128)(2,1)S(1)} %select_bitcast_fusion.q_ref.g_ref, ...), custom_call_target="tpu_custom_call", output_to_operand_aliasing={{2}: (11, {})} | custom-call | flops 8472494080 | bytes 3309568 | tf_op jit(solution)/shard_map/backward_group/pallas_call | solution.py:205
  232.9 37.2 %collective-permute-start.9 = (bf16[128,4096]{1,0:T(8,128)(2,1)S(1)}, bf16[128,4096]{1,0:T(8,128)(2,1)S(1)}, u32[]{:S(2)}, u32[]{:S(2)}) collective-permute-start(bf16[128,4096]{1,0:T(8,128)(2,1)S(1)} %fusion.2), channel_id=1, source_target_pairs={{0,4},{4,8},{8,12},{12,16},{16,20},{20,24},{24,28},{1,5},{5,9},{9,... | collective-permute-start | bytes 3145736 | tf_op jit(solution)/shard_map/ppermute | solution.py:27
  270.1 47.7 %copy.19 = bf16[2,1,1601,1024]{3,0,2,1:T(2,128)(2,1)} copy(bf16[2,1,1601,1024]{3,2,1,0:T(8,128)(2,1)} %get-tuple-element.60) | data formatting | bytes 13115392
  (70 shorter events, 20.8 us)
Async XLA Ops:
  0.6 5.0 %copy-start = (s32[8,2]{0,1:T(2,128)S(1)}, s32[8,2]{0,1:T(2,128)}, u32[]{:S(2)}) copy-start(s32[8,2]{0,1:T(2,128)} %param.10) | copy-start | bytes 196
  0.6 20.3 %copy-start.11 = (bf16[128,2048]{1,0:T(8,128)(2,1)S(1)}, bf16[128,2048]{1,0:T(8,128)(2,1)}, u32[]{:S(2)}) copy-start(bf16[128,2048]{1,0:T(8,128)(2,1)} %param.8) | copy-start | bytes 1572868
  3.7 17.3 %collective-permute-start = (bf16[128,4096]{1,0:T(8,128)(2,1)S(1)}, bf16[128,4096]{1,0:T(8,128)(2,1)S(1)}, u32[]{:S(2)}, u32[]{:S(2)}) collective-permute-start(bf16[128,4096]{1,0:T(8,128)(2,1)S(1)} %pad_maximum_fusion), channel_id=1, source_target_pairs={{4,0},{8,4},{12,8},{16,12},{20,16},{24,20},{28,24},{5,1},{9,5},{13... | collective-permute-start | bytes 3145736 | tf_op jit(solution)/shard_map/ppermute | solution.py:27
  21.4 21.7 %collective-permute-start.1 = (bf16[1,128,4096]{2,1,0:T(8,128)(2,1)S(1)}, bf16[1,128,4096]{2,1,0:T(8,128)(2,1)S(1)}, u32[]{:S(2)}, u32[]{:S(2)}) collective-permute-start(bf16[1,128,4096]{2,1,0:T(8,128)(2,1)S(1)} %select_bitcast_fusion.q_ref.g_ref), channel_id=1, source_target_pairs={{0,1},{1,2},{2,3},{3,0},{4,5},{5,6},{6,7},{7,4},{8,9},{9,10},{10,1... | collective-permute-start | bytes 3145736 | tf_op jit(solution)/shard_map/ppermute | solution.py:22
  43.1 21.1 %collective-permute-start.2 = (bf16[1,128,4096]{2,1,0:T(8,128)(2,1)S(1)}, bf16[1,128,4096]{2,1,0:T(8,128)(2,1)S(1)}, u32[]{:S(2)}, u32[]{:S(2)}) collective-permute-start(bf16[1,128,4096]{2,1,0:T(8,128)(2,1)S(1)} %collective-permute-done.1.q_ref.g_ref), channel_id=1, source_target_pairs={{0,1},{1,2},{2,3},{3,0},{4,5},{5,6},{6,7},{7,4},{8,9},{9,10},{10,1... | collective-permute-start | bytes 3145736 | tf_op jit(solution)/shard_map/ppermute | solution.py:22
  44.3 7.8 %copy-start.12 = (s32[8]{0:T(128)S(1)}, s32[8]{0:T(128)}, u32[]{:S(2)}) copy-start(s32[8]{0:T(128)} %param.11) | copy-start | bytes 100
  64.2 27.3 %collective-permute-start.3 = (bf16[1,128,4096]{2,1,0:T(8,128)(2,1)S(1)}, bf16[1,128,4096]{2,1,0:T(8,128)(2,1)S(1)}, u32[]{:S(2)}, u32[]{:S(2)}) collective-permute-start(bf16[1,128,4096]{2,1,0:T(8,128)(2,1)S(1)} %collective-permute-done.2.q_ref.g_ref), channel_id=1, source_target_pairs={{0,1},{1,2},{2,3},{3,0},{4,5},{5,6},{6,7},{7,4},{8,9},{9,10},{10,1... | collective-permute-start | bytes 3145736 | tf_op jit(solution)/shard_map/ppermute | solution.py:22
  74.3 1.0 copy-start.3
  82.4 1.0 copy-start.9
  90.5 1.0 copy-start.7
  91.5 7.1 %copy-start.1 = (bf16[1,128,4096]{2,1,0:T(8,128)(2,1)}, bf16[1,128,4096]{2,1,0:T(8,128)(2,1)S(1)}, u32[]{:S(2)}) copy-start(bf16[1,128,4096]{2,1,0:T(8,128)(2,1)S(1)} %collective-permute-done.3.q_ref.g_ref) | copy-start | bytes 3145732
  98.5 1.1 copy-start.5
  112.8 18.0 %collective-permute-start.5 = (f32[2,4,2,8,128]{4,3,2,1,0:T(8,128)}, f32[2,4,2,8,128]{4,3,2,1,0:T(8,128)S(1)}, u32[]{:S(2)}, u32[]{:S(2)}) collective-permute-start(f32[2,4,2,8,128]{4,3,2,1,0:T(8,128)} %pad_maximum_fusion.7), channel_id=1, source_target_pairs={{4,0},{8,4},{12,8},{16,12},{20,16},{24,20},{28,24},{5,1},{9,5},{13... | collective-permute-start | bytes 196616 | tf_op jit(solution)/shard_map/ppermute | solution.py:27
  115.4 16.8 %collective-permute-start.4 = (f32[2,4,2,8,128]{4,3,2,1,0:T(8,128)}, f32[2,4,2,8,128]{4,3,2,1,0:T(8,128)}, u32[]{:S(2)}, u32[]{:S(2)}) collective-permute-start(f32[2,4,2,8,128]{4,3,2,1,0:T(8,128)} %pad_maximum_fusion.6), channel_id=1, source_target_pairs={{0,4},{4,8},{8,12},{12,16},{16,20},{20,24},{24,28},{1,5},{5,9},{9,... | collective-permute-start | bytes 196616 | tf_op jit(solution)/shard_map/ppermute | solution.py:27
  134.2 3.6 %copy-start.10 = (f32[2,128,1024]{2,1,0:T(8,128)S(1)}, f32[2,128,1024]{2,1,0:T(8,128)}, u32[]{:S(2)}) copy-start(f32[2,128,1024]{2,1,0:T(8,128)} %copy-done.9) | copy-start | bytes 3145732
  149.4 15.6 %copy-start.8 = (f32[2,128,1024]{2,1,0:T(8,128)S(1)}, f32[2,128,1024]{2,1,0:T(8,128)}, u32[]{:S(2)}) copy-start(f32[2,128,1024]{2,1,0:T(8,128)} %copy-done.7) | copy-start | bytes 3145732
  149.5 15.5 %collective-permute-start.6 = (bf16[128,4096]{1,0:T(8,128)(2,1)S(1)}, bf16[128,4096]{1,0:T(8,128)(2,1)S(1)}, u32[]{:S(2)}, u32[]{:S(2)}) collective-permute-start(bf16[128,4096]{1,0:T(8,128)(2,1)S(1)} %pad_maximum_fusion.1), channel_id=1, source_target_pairs={{0,1},{1,2},{2,3},{3,0},{4,5},{5,6},{6,7},{7,4},{8,9},{9,10},{10,1... | collective-permute-start | bytes 3145736 | tf_op jit(solution)/shard_map/ppermute | solution.py:22
  176.7 15.8 %copy-start.2 = (bf16[1,128,4096]{2,1,0:T(8,128)(2,1)S(1)}, bf16[1,128,4096]{2,1,0:T(8,128)(2,1)}, u32[]{:S(2)}) copy-start(bf16[1,128,4096]{2,1,0:T(8,128)(2,1)} %copy-done.1) | copy-start | bytes 3145732
  176.8 15.8 %copy-start.6 = (f32[2,128,1024]{2,1,0:T(8,128)S(1)}, f32[2,128,1024]{2,1,0:T(8,128)}, u32[]{:S(2)}) copy-start(f32[2,128,1024]{2,1,0:T(8,128)} %copy-done.5) | copy-start | bytes 3145732
  176.8 15.7 %collective-permute-start.7 = (bf16[128,4096]{1,0:T(8,128)(2,1)S(1)}, bf16[128,4096]{1,0:T(8,128)(2,1)S(1)}, u32[]{:S(2)}, u32[]{:S(2)}) collective-permute-start(bf16[128,4096]{1,0:T(8,128)(2,1)S(1)} %pad_maximum_fusion.2), channel_id=1, source_target_pairs={{0,1},{1,2},{2,3},{3,0},{4,5},{5,6},{6,7},{7,4},{8,9},{9,10},{10,1... | collective-permute-start | bytes 3145736 | tf_op jit(solution)/shard_map/ppermute | solution.py:22
  204.4 16.4 %copy-start.4 = (f32[2,128,1024]{2,1,0:T(8,128)S(1)}, f32[2,128,1024]{2,1,0:T(8,128)}, u32[]{:S(2)}) copy-start(f32[2,128,1024]{2,1,0:T(8,128)} %copy-done.3) | copy-start | bytes 3145732
  204.4 16.3 %collective-permute-start.8 = (bf16[128,4096]{1,0:T(8,128)(2,1)S(1)}, bf16[128,4096]{1,0:T(8,128)(2,1)S(1)}, u32[]{:S(2)}, u32[]{:S(2)}) collective-permute-start(bf16[128,4096]{1,0:T(8,128)(2,1)S(1)} %pad_maximum_fusion.3), channel_id=1, source_target_pairs={{0,1},{1,2},{2,3},{3,0},{4,5},{5,6},{6,7},{7,4},{8,9},{9,10},{10,1... | collective-permute-start | bytes 3145736 | tf_op jit(solution)/shard_map/ppermute | solution.py:22
  232.9 84.9 %collective-permute-start.9 = (bf16[128,4096]{1,0:T(8,128)(2,1)S(1)}, bf16[128,4096]{1,0:T(8,128)(2,1)S(1)}, u32[]{:S(2)}, u32[]{:S(2)}) collective-permute-start(bf16[128,4096]{1,0:T(8,128)(2,1)S(1)} %fusion.2), channel_id=1, source_target_pairs={{0,4},{4,8},{8,12},{12,16},{16,20},{20,24},{24,28},{1,5},{5,9},{9,... | collective-permute-start | bytes 3145736 | tf_op jit(solution)/shard_map/ppermute | solution.py:27

commit v2 on v1

v2 whole, which is shorter than its diff:
```python
import functools

import jax
import jax.numpy as jnp
from jax import lax
from jax.experimental import pallas as pl
from jax.experimental.pallas import tpu as pltpu
from jax.sharding import PartitionSpec as P

HEAD_SIZE = 128
TILES = 4
LOW = -1e30
HIGH = 1e30
SCALE = HEAD_SIZE ** (-0.5)
LOG2E = 1.4426950408889634
BLOCK = 512
PAIR_ROWS = 256


def rotated(x, axis, by):
    total = lax.axis_size(axis)
    return lax.ppermute(x, axis, [(i, (i + by) % total) for i in range(total)])


def shifted(x, axis, by):
    total = lax.axis_size(axis)
    return lax.ppermute(x, axis, [(i, i + by) for i in range(total) if 0 <= i + by < total])


def dot_nt(a, b):
    return lax.dot_general(a, b, (((1,), (1,)), ((), ())), preferred_element_type=jnp.float32)


def dot_tn(a, b):
    return lax.dot_general(a, b, (((0,), (0,)), ((), ())), preferred_element_type=jnp.float32)


def dot_nn(a, b):
    return lax.dot_general(a, b, (((1,), (0,)), ((), ())), preferred_element_type=jnp.float32)


def stacked(ref, groups):
    return jnp.concatenate(
        [ref[0, :, i * HEAD_SIZE : (i + 1) * HEAD_SIZE] for i in range(groups)], axis=0
    )


def lanes_of(ref, groups):
    return jnp.concatenate([ref[0, i : i + 1] for i in range(groups)], axis=1)


def cuts(tokens):
    return [(start, min(BLOCK, tokens - start)) for start in range(0, tokens, BLOCK)]


def params():
    return pltpu.CompilerParams(vmem_limit_bytes=48 * 1024 * 1024)


def join_kernel(x_ref, o_ref):
    o_ref[:, 0, :] = x_ref[0]
    o_ref[:, 1, :] = x_ref[1]


def join_pairs(halves):
    _, tokens, width = halves.shape
    return pl.pallas_call(
        join_kernel,
        grid=(pl.cdiv(tokens, PAIR_ROWS),),
        in_specs=[pl.BlockSpec((2, PAIR_ROWS, width), lambda i: (0, i, 0))],
        out_specs=pl.BlockSpec((PAIR_ROWS, 2, width), lambda i: (i, 0, 0)),
        out_shape=jax.ShapeDtypeStruct((tokens, 2, width), halves.dtype),
        compiler_params=params(),
        cost_estimate=pl.CostEstimate(
            flops=0, bytes_accessed=4 * tokens * width * 4, transcendentals=0
        ),
        name="join_pairs",
    )(halves)


def forward_kernel(groups, at_ref, q_ref, k_ref, v_ref, o_ref, wide_ref, lse_ref, s_ref):
    parts = cuts(k_ref.shape[1])
    q = stacked(q_ref, groups)
    top = None
    for start, size in parts:
        s = dot_nt(k_ref[0, start : start + size], q)
        s_ref[start : start + size] = s
        peak = jnp.max(s, axis=0, keepdims=True)
        top = peak if top is None else jnp.maximum(top, peak)
    top = top * (SCALE * LOG2E)
    total = None
    out = None
    for start, size in parts:
        p = jnp.exp2(s_ref[start : start + size] * (SCALE * LOG2E) - top)
        part_total = jnp.sum(p, axis=0, keepdims=True)
        part_out = dot_tn(v_ref[0, start : start + size], p.astype(jnp.bfloat16))
        total = part_total if total is None else total + part_total
        out = part_out if out is None else out + part_out
    out = out / total
    lse = top + jnp.log2(total)
    wide_ref[0] = out
    for i in range(groups):
        span = slice(i * HEAD_SIZE, (i + 1) * HEAD_SIZE)
        o_ref[:, span] = out[:, span].T.astype(jnp.bfloat16)
        lse_ref[0, i : i + 1] = lse[:, span]


def delta_kernel(groups, at_ref, g_ref, wide_ref, delta_ref):
    for i in range(groups):
        span = slice(i * HEAD_SIZE, (i + 1) * HEAD_SIZE)
        g_t = g_ref[0, :, span].astype(jnp.float32).T
        delta_ref[0, i : i + 1] = jnp.sum(g_t * wide_ref[0, :, span], axis=0, keepdims=True)


def backward_kernel(groups, at_ref, q_ref, g_ref, k_ref, v_ref, lse_ref, delta_ref, *rest):
    dq_ref, dkv_ref = rest[-2:]
    q = stacked(q_ref, groups)
    g = stacked(g_ref, groups)
    lse = lanes_of(lse_ref, groups)
    delta = lanes_of(delta_ref, groups)
    grad_q = None
    for start, size in cuts(k_ref.shape[1]):
        k = k_ref[0, start : start + size]
        v = v_ref[0, start : start + size]
        w = jnp.exp2(dot_nt(k, q) * (SCALE * LOG2E) - lse)
        ds = (w * (dot_nt(v, g) - delta)).astype(jnp.bfloat16)
        dkv_ref[0, start : start + size] = (dot_nn(ds, q) * SCALE).astype(jnp.bfloat16)
        dkv_ref[1, start : start + size] = dot_nn(w.astype(jnp.bfloat16), g).astype(jnp.bfloat16)
        part = dot_tn(k, ds)
        grad_q = part if grad_q is None else grad_q + part
    for i in range(groups):
        span = slice(i * HEAD_SIZE, (i + 1) * HEAD_SIZE)
        dq_ref[:, span] = (grad_q[:, span] * SCALE).T


def row_spec(rows, groups):
    return pl.BlockSpec((1, rows.shape[1], groups * HEAD_SIZE), lambda h, at: (at[1], 0, h))


def image_specs(image_kv, heads):
    tokens = image_kv.shape[1]
    return [
        pl.BlockSpec((1, tokens, HEAD_SIZE), lambda h, at: (0, 0, at[0] * heads + h)),
        pl.BlockSpec((1, tokens, HEAD_SIZE), lambda h, at: (1, 0, at[0] * heads + h)),
    ]


def stat_spec(groups, text):
    return pl.BlockSpec((1, groups, text), lambda h, *at: (h, 0, 0))


def forward_call(at, q, image_kv, groups, heads):
    text = q.shape[1]
    width = groups * HEAD_SIZE
    tokens = image_kv.shape[1]
    lanes = groups * text
    return pl.pallas_call(
        functools.partial(forward_kernel, groups),
        grid_spec=pltpu.PrefetchScalarGridSpec(
            num_scalar_prefetch=1,
            grid=(heads,),
            in_specs=[row_spec(q, groups)] + image_specs(image_kv, heads),
            out_specs=[
                pl.BlockSpec((text, width), lambda h, at: (0, h)),
                pl.BlockSpec((1, HEAD_SIZE, lanes), lambda h, at: (h, 0, 0)),
                stat_spec(groups, text),
            ],
            scratch_shapes=[pltpu.VMEM((tokens + (-tokens) % 8, lanes), jnp.float32)],
        ),
        out_shape=[
            jax.ShapeDtypeStruct((text, heads * width), jnp.bfloat16),
            jax.ShapeDtypeStruct((heads, HEAD_SIZE, lanes), jnp.float32),
            jax.ShapeDtypeStruct((heads, groups, text), jnp.float32),
        ],
        compiler_params=params(),
        cost_estimate=pl.CostEstimate(
            flops=heads * 8 * tokens * lanes * HEAD_SIZE,
            bytes_accessed=heads * tokens * HEAD_SIZE * 4,
            transcendentals=heads * tokens * lanes,
        ),
        name="forward_group",
    )(at, q, image_kv, image_kv)


def delta_call(at, g, wide, groups, heads):
    text = g.shape[1]
    lanes = groups * text
    return pl.pallas_call(
        functools.partial(delta_kernel, groups),
        grid_spec=pltpu.PrefetchScalarGridSpec(
            num_scalar_prefetch=1,
            grid=(heads,),
            in_specs=[row_spec(g, groups), pl.BlockSpec((1, HEAD_SIZE, lanes), lambda h, at: (h, 0, 0))],
            out_specs=stat_spec(groups, text),
        ),
        out_shape=jax.ShapeDtypeStruct((heads, groups, text), jnp.float32),
        compiler_params=params(),
        cost_estimate=pl.CostEstimate(
            flops=heads * 2 * lanes * HEAD_SIZE, bytes_accessed=heads * lanes * HEAD_SIZE * 6, transcendentals=0
        ),
        name="delta_group",
    )(at, g, wide)


def backward_call(at, q, g, image_kv, lse, delta, grads, groups, heads):
    text = q.shape[1]
    width = groups * HEAD_SIZE
    tokens = image_kv.shape[1]
    lanes = groups * text
    stat = stat_spec(groups, text)
    in_specs = [row_spec(q, groups), row_spec(g, groups)] + image_specs(image_kv, heads) + [stat, stat]
    operands = [at, q, g, image_kv, image_kv, lse, delta]
    aliases = {}
    if grads is not None:
        in_specs.append(pl.BlockSpec(memory_space=pl.ANY))
        aliases = {len(operands): 1}
        operands.append(grads)
    return pl.pallas_call(
        functools.partial(backward_kernel, groups),
        grid_spec=pltpu.PrefetchScalarGridSpec(
            num_scalar_prefetch=1,
            grid=(heads,),
            in_specs=in_specs,
            out_specs=[
                pl.BlockSpec((text, width), lambda h, at: (0, h)),
                pl.BlockSpec((2, tokens, HEAD_SIZE), lambda h, at: (0, 0, at[0] * heads + h)),
            ],
        ),
        out_shape=[
            jax.ShapeDtypeStruct((text, heads * width), jnp.float32),
            jax.ShapeDtypeStruct(image_kv.shape, jnp.bfloat16),
        ],
        input_output_aliases=aliases,
        compiler_params=params(),
        cost_estimate=pl.CostEstimate(
            flops=heads * 20 * tokens * lanes * HEAD_SIZE,
            bytes_accessed=heads * tokens * HEAD_SIZE * 8,
            transcendentals=heads * tokens * lanes,
        ),
        name="backward_group",
    )(*operands)


def mix_kernel(groups, o_ref, own_ref, old_ref, carried_ref, out_ref):
    own = own_ref[0].T
    old = old_ref[0].T
    for i in range(groups):
        span = slice(i * HEAD_SIZE, (i + 1) * HEAD_SIZE)
        mix = o_ref[:, span].astype(jnp.float32) * own[:, i : i + 1]
        mix = mix + carried_ref[:, span].astype(jnp.float32) * old[:, i : i + 1]
        out_ref[:, span] = mix.astype(jnp.bfloat16)


def mix_call(out, own, old, carried):
    heads, groups, text = own.shape
    width = groups * HEAD_SIZE
    rows = pl.BlockSpec((text, width), lambda h: (0, h))
    return pl.pallas_call(
        functools.partial(mix_kernel, groups),
        grid=(heads,),
        in_specs=[rows, stat_spec(groups, text), stat_spec(groups, text), rows],
        out_specs=rows,
        out_shape=jax.ShapeDtypeStruct((text, heads * width), jnp.bfloat16),
        compiler_params=params(),
        cost_estimate=pl.CostEstimate(
            flops=4 * text * heads * width, bytes_accessed=6 * text * heads * width, transcendentals=0
        ),
        name="mix_group",
    )(out, own, old, carried)


def merged(lse, delta):
    top = jnp.max(lse, axis=0)
    share = jnp.exp2(lse - top)
    total = jnp.sum(share, axis=0)
    return top + jnp.log2(total), jnp.sum(share * delta, axis=0) / total


def shards(queries, image_key_value, image_spans, tile_counts, cross_gate, grad_out):
    seq_index = lax.axis_index("seq")
    seq_total = lax.axis_size("seq")
    enc_index = lax.axis_index("enc")
    enc_total = lax.axis_size("enc")
    text, width = queries.shape
    heads = image_key_value.shape[3] // (enc_total * HEAD_SIZE)
    groups = width // (heads * HEAD_SIZE)
    row_images = enc_total // TILES
    gate = jnp.tanh(cross_gate[0])
    steps = range(enc_total)

    spans = lax.dynamic_slice_in_dim(image_spans, seq_index * row_images, row_images, 0)
    offsets = spans[:, 0] - seq_index * text
    slots = jnp.arange(text, dtype=jnp.int32)
    in_own = slots[None, :] >= offsets[:, None]
    positions = jnp.where(in_own, seq_index * text, (seq_index + 1) * text) + slots[None, :]
    seen = (positions >= spans[:, :1]) & (positions < spans[:, 1:])

    sources = [lax.rem(enc_index - step + enc_total, enc_total) for step in steps]
    places = [source // TILES for source in sources]
    ats = [jnp.stack([source, places[0]]).astype(jnp.int32) for source in sources]
    counts = lax.dynamic_slice_in_dim(tile_counts, seq_index * row_images, row_images, 0)

    def of_place(x):
        return x[0] if row_images == 1 else lax.dynamic_index_in_dim(x, places[0], 0, False)

    def of_group(x, step):
        return lax.dynamic_index_in_dim(x, sources[step], 0, False)

    def placed(message, carried):
        if row_images == 1:
            return message
        base = jnp.zeros((row_images,) + message.shape, message.dtype) if carried is None else carried
        return lax.dynamic_update_index_in_dim(base, message, places[0], 0)

    in_use = (enc_index - places[0] * TILES) < of_place(counts)
    my_seen = of_place(seen) & in_use
    wide_own = in_own[:, None, None, None, :]
    order = jnp.stack(sources)

    def window(own, later):
        return jnp.where(in_own[:, :, None], own[None], later[None])

    grad_mixed = (gate * grad_out.astype(jnp.float32)).astype(jnp.bfloat16)
    q_moving = window(queries, shifted(queries, "seq", -1))
    q_first, g_later = lax.optimization_barrier((q_moving, shifted(grad_mixed, "seq", -1)))
    q_rings = [q_first]
    g_rings = [window(grad_mixed, g_later)]
    image_kv = image_key_value[:, 0]
    outs, wides, lse_ring, delta_ring = [], [], [], []
    for step in steps:
        more = step + 1 < enc_total
        if more:
            q_next = rotated(q_moving if step == 0 else q_rings[step], "enc", 1)
            if step == 0:
                q_next, image_kv = lax.optimization_barrier((q_next, image_kv))
            q_rings.append(q_next)
        out, wide, lse = forward_call(ats[step], q_rings[step], image_kv, groups, heads)
        outs.append(out)
        wides.append(wide)
        if step > 0:
            g_next, lse = lax.optimization_barrier((g_next, lse))
            g_rings.append(g_next)
        lse_ring.append(lse)
        if more:
            g_next = rotated(g_rings[step], "enc", 1)
        delta_ring.append(delta_call(ats[step], g_rings[step], wides[step], groups, heads))

    lse_mine = jnp.take(jnp.where(my_seen, jnp.stack(lse_ring), LOW), order, axis=0)
    delta_mine = jnp.take(jnp.stack(delta_ring), order, axis=0)
    mine = jnp.stack([lse_mine, delta_mine])
    early = row_images == 1
    tiles = [mine] + [rotated(mine, "enc", step) for step in steps[1:]]
    tile_lse = jnp.stack([t[0] for t in tiles])
    tile_delta = jnp.stack([t[1] for t in tiles])
    if early:
        first_out, tile_lse = lax.optimization_barrier((outs[1], tile_lse))
        mix_carried = rotated(first_out, "enc", 1)
    image_lse, image_delta = [], []
    for a in range(row_images):
        lse_a = tile_lse
        if row_images > 1:
            lse_a = jnp.where((jnp.stack(places) == a)[:, None, None, None, None], lse_a, LOW)
        lse_a, delta_a = merged(lse_a, tile_delta)
        image_lse.append(lse_a)
        image_delta.append(delta_a)
    image_lse, image_delta = jnp.stack(image_lse), jnp.stack(image_delta)
    upper = merged(jnp.where(wide_own, image_lse, LOW), image_delta)
    lower = merged(jnp.where(wide_own, LOW, image_lse), image_delta)
    lower, upper = lax.optimization_barrier((jnp.stack(lower), jnp.stack(upper)))
    from_before = shifted(lower, "seq", 1)
    from_after = shifted(upper, "seq", -1)
    if early:
        from_before, from_after, mix_carried = lax.optimization_barrier((from_before, from_after, mix_carried))
    before_lse = jnp.where(seq_index > 0, from_before[0], LOW)
    after_lse = jnp.where(seq_index < seq_total - 1, from_after[0], LOW)
    own_total = merged(jnp.stack([upper[0], before_lse]), jnp.stack([upper[1], from_before[1]]))
    next_total = merged(jnp.stack([lower[0], after_lse]), jnp.stack([lower[1], from_after[1]]))
    full_lse = jnp.where(wide_own, own_total[0], next_total[0])
    full_delta = jnp.where(wide_own, own_total[1], next_total[1])
    mine_share = jnp.where(my_seen, jnp.exp2(lse_mine - of_place(image_lse)), 0.0)
    home_share = jnp.where(full_lse > LOW / 2, jnp.exp2(image_lse - full_lse), 0.0) * gate
    lse_used = jnp.where(my_seen, of_place(full_lse), HIGH)
    delta_used = of_place(full_delta)

    def mixed(step, carried):
        share = of_group(mine_share, step)
        if carried is None:
            return mix_call(outs[step], share, share, jnp.zeros((text, width), jnp.bfloat16))
        old = jnp.ones_like(share)
        if early and step == 2:
            old = jnp.exp2(of_group(tile_lse[1], step) - of_group(of_place(image_lse), step))
        if early and step == 0:
            home = of_group(home_share[0], 0)
            share, old = share * home, old * home
        return mix_call(outs[step], share, old, of_place(carried) if row_images > 1 else carried)

    def homing(sums):
        sums = sums.reshape(row_images, text, width).astype(jnp.float32)
        kept = jnp.sum(jnp.where(in_own[:, :, None], sums, 0.0), axis=0)
        passed = jnp.sum(jnp.where(in_own[:, :, None], 0.0, sums), axis=0).astype(jnp.bfloat16)
        return kept, shifted(passed, "seq", 1)

    def homed(kept, passed):
        return (kept + passed.astype(jnp.float32)).astype(jnp.bfloat16)

    def scaled_home(sums):
        if early:
            return sums
        shares = jnp.stack([of_group(home_share[a], 0) for a in range(row_images)])
        shares = shares.reshape(row_images, heads * groups, text).transpose(0, 2, 1)
        parts = sums.reshape(row_images, text, heads * groups, HEAD_SIZE).astype(jnp.float32)
        return (parts * shares[..., None]).reshape(row_images, text, width).astype(jnp.bfloat16)

    if not early:
        mix_carried = rotated(placed(mixed(1, None), None), "enc", 1)
    mix_carried = placed(mixed(2, mix_carried), mix_carried)
    mix_moving = rotated(mix_carried, "enc", 1)
    grads = None
    carried = None
    for step in list(steps[1:]) + [0]:
        q = q_rings[step]
        grad_q, grads = backward_call(
            ats[step], q, g_rings[step], image_kv, of_group(lse_used, step), of_group(delta_used, step),
            grads, groups, heads,
        )
        if step == 0:
            grad_q, mix_passed = lax.optimization_barrier((grad_q, mix_passed))
        if carried is not None:
            grad_q = grad_q + (carried if row_images == 1 else of_place(carried)).astype(jnp.float32)
        carried = placed(grad_q.astype(jnp.bfloat16), carried)
        if step > 0:
            carried = rotated(carried, "enc", 1)
        following = 0 if step + 2 > enc_total else step + 2
        if 0 < step and (step + 2) <= enc_total:
            mix_moving, grads = lax.optimization_barrier((mix_moving, grads))
            mix_carried = placed(mixed(following % enc_total, mix_moving), mix_moving)
            if following % enc_total:
                mix_moving = rotated(mix_carried, "enc", 1)
            else:
                mix_kept, mix_passed = homing(scaled_home(mix_carried))
    grads = join_pairs(grads).transpose(1, 0, 2).reshape(image_key_value.shape)

    grad_kept, grad_passed = homing(carried)
    return (homed(mix_kept, mix_passed), homed(grad_kept, grad_passed), grads)


def solution(mesh):
    in_specs = (
        P("seq", "enc"),
        P(None, ("seq", "enc"), None, None),
        P(),
        P(),
        P(),
        P("seq", "enc"),
    )
    out_specs = (P("seq", "enc"), P("seq", "enc"), P(None, ("seq", "enc"), None, None))
    return jax.shard_map(shards, mesh=mesh, in_specs=in_specs, out_specs=out_specs, check_vma=False)
```

time: 323 us -> 207 us (0.64)
  local copies, waits for them, and re-layouts: 73.2 us -> 13.8 us
  starting transfers between devices: 61.4 us -> 32.5 us
  waiting for transfers between devices: 86.5 us -> 59.3 us
  Pallas kernels: 75.3 us -> 90.4 us
  blocking collectives: 11.1 us -> 0 us
    unnamed x28 -> x29, local copies, waits for them, and re-layouts: 59.4 us -> 10.7 us
    ppermute x4 -> x6, starting transfers between devices: 56.5 us -> 23.8 us  [shifted(): lax.ppermute(x, axis, [(i, i + by) for i in range(total) if 0 <= i + by <...]
    pallas_call x8 -> x16, Pallas kernels: 75.3 us -> 90.4 us  [the longest x4 46.3 us: backward_call(): pl.pallas_call(functools.partial(backward_kernel, groups), grid_spec=pltp...]
    ppermute x6 -> x15, waiting for transfers between devices: 71.1 us -> 56.2 us  [rotated(): return lax.ppermute(x, axis, [(i, (i + by) % total) for i in range(total)])]
    ppermute x4 -> x6, waiting for transfers between devices: 15.4 us -> 3.13 us  [shifted(): lax.ppermute(x, axis, [(i, i + by) for i in range(total) if 0 <= i + by <...]
    all_gather x1 -> x0, blocking collectives: 11.1 us -> none  [shards(): gathered = lax.all_gather(jnp.stack([lse_all, delta_all]), 'enc')]
    pad x1 -> x0, local copies, waits for them, and re-layouts: 6.66 us -> none  [shards(): image_kv = jnp.pad(image_key_value, ((0, 0), (0, 0), (0, padding), (0, 0)))]
    ppermute x6 -> x15, starting transfers between devices: 4.91 us -> 8.69 us  [rotated(): return lax.ppermute(x, axis, [(i, (i + by) % total) for i in range(total)])]
  transfers between devices with their start and end apart: 10 -> 21, of which waited for: 7 -> 16; matrix products, arithmetic and copies ran while one was open for 21% -> 6% of each run, Pallas kernels for 7% -> 43%
where the time goes in v2:
time: 207 us; the launch traced here: 206 us
  Pallas kernels  90.4 us (44%)
  waiting for transfers between devices  59.3 us (29%)
  starting transfers between devices  32.5 us (16%)
  local copies, waits for them, and re-layouts  13.8 us (7%)
  other arithmetic  6.75 us (3%)
  between operations  3.17 us (2%)
    ppermute x15, waiting for transfers between devices, rotated(): return lax.ppermute(x, axis, [(i, (i + by) % total) for i in range(total)])  56.2 us
    pallas_call x4, Pallas kernels, backward_call(): pl.pallas_call(functools.partial(backward_kernel, groups), grid_spec=pltp...  46.3 us
    pallas_call x4, Pallas kernels, forward_call(): pl.pallas_call(functools.partial(forward_kernel, groups), grid_spec=pltpu...  27.8 us
    ppermute x6, starting transfers between devices, shifted(): lax.ppermute(x, axis, [(i, i + by) for i in range(total) if 0 <= i + by <...  23.8 us
    unnamed x29, local copies, waits for them, and re-layouts  10.7 us
    pallas_call x1, Pallas kernels, join_pairs(): pl.pallas_call(join_kernel, grid=(pl.cdiv(tokens, PAIR_ROWS),), in_specs=...  9.06 us
    ppermute x15, starting transfers between devices, rotated(): return lax.ppermute(x, axis, [(i, (i + by) % total) for i in range(total)])  8.69 us
  transfers between devices with their start and end apart: 21, of which 16 were waited for; matrix products, arithmetic and copies ran while one was open for 6% of the time, Pallas kernels for 43%

profile of v2, /device:TPU:1, one launch (start us, length us, event | category | flops | bytes accessed | tf_op | source)
XLA Modules:
  0.0 205.9 jit_solution(13855737278038588730)
XLA Ops:
  9.3 7.8 %copy.14 = bf16[2,1,1601,1024]{3,2,0,1:T(8,128)(2,1)} copy(bf16[2,1,1601,1024]{3,0,2,1:T(2,128)(2,1)} %param.9) | data formatting | bytes 13115392 | tf_op args[1]
  23.7 11.8 %collective-permute-done.2.q_ref = bf16[1,128,2048]{2,1,0:T(8,128)(2,1)S(1)} collective-permute-done((bf16[1,128,2048]{2,1,0:T(8,128)(2,1)S(1)}, bf16[1,128,2048]{2,1,0:T(8,128)(2,1)S(1)}, u32[]{:S(2)}, u32[]{:S(2)}) %collective-permute-start.2) | collective-permute-done | bytes 524320 | tf_op jit(solution)/shard_map/ppermute | solution.py:22
  35.5 7.0 %forward_group.5 = (bf16[128,2048]{1,0:T(8,128)(2,1)S(1)}, f32[2,128,1024]{2,1,0:T(8,128)S(1)}, f32[2,8,128]{2,1,0:T(8,128)S(1)}) custom-call(s32[2]{0:T(128)S(1)} %pad_add_fusion.1.at_ref, bf16[1,128,2048]{2,1,0:T(8,128)(2,1)S(1)} %collective-permute-done.2.q_ref, bf16[2,1601,1024]{2,1,0:T(8,128)(2,1)} %bitcast.103, bf16[2,1601,1024]{2,1,0:T(8,128)(2,1)} %bitcast.104), custom_call_target="tpu_custom_call" | custom-call | flops 3357540352 | bytes 1639424 | tf_op jit(solution)/shard_map/forward_group/pallas_call | solution.py:157
  43.4 3.4 %collective-permute-done.3.g_ref = bf16[1,128,2048]{2,1,0:T(8,128)(2,1)S(1)} collective-permute-done((bf16[1,128,2048]{2,1,0:T(8,128)(2,1)S(1)}, bf16[1,128,2048]{2,1,0:T(8,128)(2,1)S(1)}, u32[]{:S(2)}, u32[]{:S(2)}) %collective-permute-start.3) | collective-permute-done | bytes 524320 | tf_op jit(solution)/shard_map/ppermute | solution.py:22
  49.0 9.0 %collective-permute-done.5.q_ref = bf16[1,128,2048]{2,1,0:T(8,128)(2,1)S(1)} collective-permute-done((bf16[1,128,2048]{2,1,0:T(8,128)(2,1)S(1)}, bf16[1,128,2048]{2,1,0:T(8,128)(2,1)S(1)}, u32[]{:S(2)}, u32[]{:S(2)}) %collective-permute-start.5) | collective-permute-done | bytes 524320 | tf_op jit(solution)/shard_map/ppermute | solution.py:22
  58.0 7.0 %forward_group.6 = (bf16[128,2048]{1,0:T(8,128)(2,1)S(1)}, f32[2,128,1024]{2,1,0:T(8,128)S(1)}, f32[2,8,128]{2,1,0:T(8,128)S(1)}) custom-call(s32[2]{0:T(128)S(1)} %pad_add_fusion.2.at_ref, bf16[1,128,2048]{2,1,0:T(8,128)(2,1)S(1)} %collective-permute-done.5.q_ref, bf16[2,1601,1024]{2,1,0:T(8,128)(2,1)} %bitcast.105, bf16[2,1601,1024]{2,1,0:T(8,128)(2,1)} %bitcast.106), custom_call_target="tpu_custom_call" | custom-call | flops 3357540352 | bytes 1639424 | tf_op jit(solution)/shard_map/forward_group/pallas_call | solution.py:157
  65.0 4.2 %collective-permute-done.4.g_ref = bf16[1,128,2048]{2,1,0:T(8,128)(2,1)S(1)} collective-permute-done((bf16[1,128,2048]{2,1,0:T(8,128)(2,1)S(1)}, bf16[1,128,2048]{2,1,0:T(8,128)(2,1)S(1)}, u32[]{:S(2)}, u32[]{:S(2)}) %collective-permute-start.4) | collective-permute-done | bytes 524320 | tf_op jit(solution)/shard_map/ppermute | solution.py:22
  69.2 7.0 %forward_group.4 = (bf16[128,2048]{1,0:T(8,128)(2,1)S(1)}, f32[2,128,1024]{2,1,0:T(8,128)S(1)}, f32[2,8,128]{2,1,0:T(8,128)S(1)}) custom-call(s32[2]{0:T(128)S(1)} %pad_add_fusion.at_ref, bf16[1,128,2048]{2,1,0:T(8,128)(2,1)S(1)} %select_bitcast_fusion.1.q_ref, bf16[2,1601,1024]{2,1,0:T(8,128)(2,1)} %bitcast.107, bf16[2,1601,1024]{2,1,0:T(8,128)(2,1)} %bitcast.108), custom_call_target="tpu_custom_call" | custom-call | flops 3357540352 | bytes 1639424 | tf_op jit(solution)/shard_map/forward_group/pallas_call | solution.py:157
  78.1 2.4 %collective-permute-done.7.q_ref = bf16[1,128,2048]{2,1,0:T(8,128)(2,1)S(1)} collective-permute-done((bf16[1,128,2048]{2,1,0:T(8,128)(2,1)S(1)}, bf16[1,128,2048]{2,1,0:T(8,128)(2,1)S(1)}, u32[]{:S(2)}, u32[]{:S(2)}) %collective-permute-start.7) | collective-permute-done | bytes 524320 | tf_op jit(solution)/shard_map/ppermute | solution.py:22
  80.5 7.0 %forward_group.7 = (bf16[128,2048]{1,0:T(8,128)(2,1)S(1)}, f32[2,128,1024]{2,1,0:T(8,128)S(1)}, f32[2,8,128]{2,1,0:T(8,128)S(1)}) custom-call(s32[2]{0:T(128)S(1)} %pad_add_fusion.3.at_ref, bf16[1,128,2048]{2,1,0:T(8,128)(2,1)S(1)} %collective-permute-done.7.q_ref, bf16[2,1601,1024]{2,1,0:T(8,128)(2,1)} %bitcast.109, bf16[2,1601,1024]{2,1,0:T(8,128)(2,1)} %bitcast.110), custom_call_target="tpu_custom_call" | custom-call | flops 3357540352 | bytes 1639424 | tf_op jit(solution)/shard_map/forward_group/pallas_call | solution.py:157
  87.4 2.5 %collective-permute-done.6.g_ref = bf16[1,128,2048]{2,1,0:T(8,128)(2,1)S(1)} collective-permute-done((bf16[1,128,2048]{2,1,0:T(8,128)(2,1)S(1)}, bf16[1,128,2048]{2,1,0:T(8,128)(2,1)S(1)}, u32[]{:S(2)}, u32[]{:S(2)}) %collective-permute-start.6) | collective-permute-done | bytes 524320 | tf_op jit(solution)/shard_map/ppermute | solution.py:22
  95.8 5.2 %collective-permute-done.9 = f32[2,4,2,8,128]{4,3,2,1,0:T(8,128)S(1)} collective-permute-done((f32[2,4,2,8,128]{4,3,2,1,0:T(8,128)S(1)}, f32[2,4,2,8,128]{4,3,2,1,0:T(8,128)S(1)}, u32[]{:S(2)}, u32[]{:S(2)}) %collective-permute-start.9) | collective-permute-done | bytes 65568 | tf_op jit(solution)/shard_map/ppermute | solution.py:22
  101.4 2.3 %collective-permute-start.12 = (f32[2,4,2,8,128]{4,3,2,1,0:T(8,128)S(1)}, f32[2,4,2,8,128]{4,3,2,1,0:T(8,128)S(1)}, u32[]{:S(2)}, u32[]{:S(2)}) collective-permute-start(f32[2,4,2,8,128]{4,3,2,1,0:T(8,128)S(1)} %get-tuple-element.68), channel_id=1, source_target_pairs={{4,0},{8,4},{12,8},{16,12},{20,16},{24,20},{28,24},{5,1},{9,5},{13... | collective-permute-start | bytes 196616 | tf_op jit(solution)/shard_map/ppermute | solution.py:27
  103.7 5.1 %collective-permute-start.11 = (f32[2,4,2,8,128]{4,3,2,1,0:T(8,128)S(1)}, f32[2,4,2,8,128]{4,3,2,1,0:T(8,128)S(1)}, u32[]{:S(2)}, u32[]{:S(2)}) collective-permute-start(f32[2,4,2,8,128]{4,3,2,1,0:T(8,128)S(1)} %get-tuple-element.69), channel_id=1, source_target_pairs={{0,4},{4,8},{8,12},{12,16},{16,20},{20,24},{24,28},{1,5},{5,9},{9,... | collective-permute-start | bytes 196616 | tf_op jit(solution)/shard_map/ppermute | solution.py:27
  110.1 6.3 %collective-permute-done.13.carried_ref = bf16[128,2048]{1,0:T(8,128)(2,1)S(1)} collective-permute-done((bf16[128,2048]{1,0:T(8,128)(2,1)}, bf16[128,2048]{1,0:T(8,128)(2,1)S(1)}, u32[]{:S(2)}, u32[]{:S(2)}) %collective-permute-start.13) | collective-permute-done | bytes 524320 | tf_op jit(solution)/shard_map/ppermute | solution.py:22
  119.9 11.6 %backward_group.4 = (f32[128,2048]{1,0:T(8,128)S(1)}, bf16[2,1601,1024]{2,1,0:T(8,128)(2,1)}) custom-call(s32[2]{0:T(128)S(1)} %pad_add_fusion.1.at_ref, bf16[1,128,2048]{2,1,0:T(8,128)(2,1)S(1)} %copy-done.10, bf16[1,128,2048]{2,1,0:T(8,128)(2,1)S(1)} %copy-done.4, bf16[2,1601,1024]{2,1,0:T(8,128)(2,1)} %bitcast.111, bf16[2,1601,1024]{2,1,0:T(8,128)(2,1)} %bitcast.112, ...), custom_call_target="tpu_custom_call" | custom-call | flops 8393850880 | bytes 3278848 | tf_op jit(solution)/shard_map/backward_group/pallas_call | solution.py:218
  133.3 11.5 %backward_group.5 = (f32[128,2048]{1,0:T(8,128)S(1)}, bf16[2,1601,1024]{2,1,0:T(8,128)(2,1)}) custom-call(s32[2]{0:T(128)S(1)} %pad_add_fusion.2.at_ref, bf16[1,128,2048]{2,1,0:T(8,128)(2,1)S(1)} %copy-done.8, bf16[1,128,2048]{2,1,0:T(8,128)(2,1)S(1)} %copy-done.2, bf16[2,1601,1024]{2,1,0:T(8,128)(2,1)} %bitcast.113, ...), custom_call_target="tpu_custom_call", output_to_operand_aliasing={{1}: (7, {})} | custom-call | flops 8393850880 | bytes 3278848 | tf_op jit(solution)/shard_map/backward_group/pallas_call | solution.py:218
  145.7 3.0 %collective-permute-start.18 = (bf16[128,2048]{1,0:T(8,128)(2,1)S(1)}, bf16[128,2048]{1,0:T(8,128)(2,1)S(1)}, u32[]{:S(2)}, u32[]{:S(2)}) collective-permute-start(bf16[128,2048]{1,0:T(8,128)(2,1)S(1)} %add_convert_fusion.2), channel_id=1, source_target_pairs={{0,1},{1,2},{2,3},{3,0},{4,5},{5,6},{6,7},{7,4},{8,9},{9,10},{10,1... | collective-permute-start | bytes 1572872 | tf_op jit(solution)/shard_map/ppermute | solution.py:22
  148.6 8.2 %collective-permute-done.15.carried_ref = bf16[128,2048]{1,0:T(8,128)(2,1)S(1)} collective-permute-done((bf16[128,2048]{1,0:T(8,128)(2,1)S(1)}, bf16[128,2048]{1,0:T(8,128)(2,1)S(1)}, u32[]{:S(2)}, u32[]{:S(2)}) %collective-permute-start.15) | collective-permute-done | bytes 524320 | tf_op jit(solution)/shard_map/ppermute | solution.py:22
  158.1 8.7 %collective-permute-start.16 = (bf16[128,2048]{1,0:T(8,128)(2,1)S(1)}, bf16[128,2048]{1,0:T(8,128)(2,1)S(1)}, u32[]{:S(2)}, u32[]{:S(2)}) collective-permute-start(bf16[128,2048]{1,0:T(8,128)(2,1)S(1)} %fusion.2), channel_id=1, source_target_pairs={{0,4},{4,8},{8,12},{12,16},{16,20},{20,24},{24,28},{1,5},{5,9},{9,... | collective-permute-start | bytes 1572872 | tf_op jit(solution)/shard_map/ppermute | solution.py:27
  166.8 11.5 %backward_group.6 = (f32[128,2048]{1,0:T(8,128)S(1)}, bf16[2,1601,1024]{2,1,0:T(8,128)(2,1)}) custom-call(s32[2]{0:T(128)S(1)} %pad_add_fusion.3.at_ref, bf16[1,128,2048]{2,1,0:T(8,128)(2,1)S(1)} %copy-done.6, bf16[1,128,2048]{2,1,0:T(8,128)(2,1)S(1)} %collective-permute-done.6.g_ref, ...), custom_call_target="tpu_custom_call", output_to_operand_aliasing={{1}: (7, {})} | custom-call | flops 8393850880 | bytes 3278848 | tf_op jit(solution)/shard_map/backward_group/pallas_call | solution.py:218
  178.8 11.6 %backward_group.7 = (f32[128,2048]{1,0:T(8,128)S(1)}, bf16[2,1601,1024]{2,1,0:T(8,128)(2,1)}) custom-call(s32[2]{0:T(128)S(1)} %pad_add_fusion.at_ref, bf16[1,128,2048]{2,1,0:T(8,128)(2,1)S(1)} %select_bitcast_fusion.1.q_ref, bf16[1,128,2048]{2,1,0:T(8,128)(2,1)S(1)} %select_bitcast_fusion.g_ref, ...), custom_call_target="tpu_custom_call", output_to_operand_aliasing={{1}: (7, {})} | custom-call | flops 8393850880 | bytes 3278848 | tf_op jit(solution)/shard_map/backward_group/pallas_call | solution.py:218
  191.5 3.8 %collective-permute-start.20 = (bf16[128,2048]{1,0:T(8,128)(2,1)S(1)}, bf16[128,2048]{1,0:T(8,128)(2,1)S(1)}, u32[]{:S(2)}, u32[]{:S(2)}) collective-permute-start(bf16[128,2048]{1,0:T(8,128)(2,1)S(1)} %fusion.5), channel_id=1, source_target_pairs={{0,4},{4,8},{8,12},{12,16},{16,20},{20,24},{24,28},{1,5},{5,9},{9,... | collective-permute-start | bytes 1572872 | tf_op jit(solution)/shard_map/ppermute | solution.py:27
  195.3 9.1 %join_pairs.1 = bf16[1601,2,1024]{2,1,0:T(2,128)(2,1)} custom-call(bf16[2,1601,1024]{2,1,0:T(8,128)(2,1)} %get-tuple-element.89.x_ref), custom_call_target="tpu_custom_call" | custom-call | bytes 26230784 | tf_op jit(solution)/shard_map/join_pairs/pallas_call | solution.py:67
  (111 shorter events, 36.1 us)
Async XLA Ops:
  2.5 18.5 %collective-permute-start.1 = (bf16[128,2048]{1,0:T(8,128)(2,1)S(1)}, bf16[128,2048]{1,0:T(8,128)(2,1)}, u32[]{:S(2)}, u32[]{:S(2)}) collective-permute-start(bf16[128,2048]{1,0:T(8,128)(2,1)S(1)} %multiply_convert_fusion), channel_id=1, source_target_pairs={{4,0},{8,4},{12,8},{16,12},{20,16},{24,20},{28,24},{5,1},{9,5},{13... | collective-permute-start | bytes 1572872 | tf_op jit(solution)/shard_map/ppermute | solution.py:27
  4.5 15.0 %collective-permute-start = (bf16[128,2048]{1,0:T(8,128)(2,1)}, bf16[128,2048]{1,0:T(8,128)(2,1)S(1)}, u32[]{:S(2)}, u32[]{:S(2)}) collective-permute-start(bf16[128,2048]{1,0:T(8,128)(2,1)} %param.8), channel_id=1, source_target_pairs={{4,0},{8,4},{12,8},{16,12},{20,16},{24,20},{28,24},{5,1},{9,5},{13... | collective-permute-start | bytes 1572872 | tf_op jit(solution)/shard_map/ppermute | solution.py:27
  19.6 15.9 %collective-permute-start.2 = (bf16[1,128,2048]{2,1,0:T(8,128)(2,1)S(1)}, bf16[1,128,2048]{2,1,0:T(8,128)(2,1)S(1)}, u32[]{:S(2)}, u32[]{:S(2)}) collective-permute-start(bf16[1,128,2048]{2,1,0:T(8,128)(2,1)S(1)} %select_bitcast_fusion.1.q_ref), channel_id=1, source_target_pairs={{0,1},{1,2},{2,3},{3,0},{4,5},{5,6},{6,7},{7,4},{8,9},{9,10},{10,1... | collective-permute-start | bytes 1572872 | tf_op jit(solution)/shard_map/ppermute | solution.py:22
  22.2 24.5 %collective-permute-start.3 = (bf16[1,128,2048]{2,1,0:T(8,128)(2,1)S(1)}, bf16[1,128,2048]{2,1,0:T(8,128)(2,1)S(1)}, u32[]{:S(2)}, u32[]{:S(2)}) collective-permute-start(bf16[1,128,2048]{2,1,0:T(8,128)(2,1)S(1)} %select_bitcast_fusion.g_ref), channel_id=1, source_target_pairs={{0,1},{1,2},{2,3},{3,0},{4,5},{5,6},{6,7},{7,4},{8,9},{9,10},{10,1... | collective-permute-start | bytes 1572872 | tf_op jit(solution)/shard_map/ppermute | solution.py:22
  35.5 22.5 %collective-permute-start.5 = (bf16[1,128,2048]{2,1,0:T(8,128)(2,1)S(1)}, bf16[1,128,2048]{2,1,0:T(8,128)(2,1)S(1)}, u32[]{:S(2)}, u32[]{:S(2)}) collective-permute-start(bf16[1,128,2048]{2,1,0:T(8,128)(2,1)S(1)} %collective-permute-done.2.q_ref), channel_id=1, source_target_pairs={{0,1},{1,2},{2,3},{3,0},{4,5},{5,6},{6,7},{7,4},{8,9},{9,10},{10,1... | collective-permute-start | bytes 1572872 | tf_op jit(solution)/shard_map/ppermute | solution.py:22
  46.8 18.2 %copy-start.3 = (bf16[1,128,2048]{2,1,0:T(8,128)(2,1)}, bf16[1,128,2048]{2,1,0:T(8,128)(2,1)S(1)}, u32[]{:S(2)}) copy-start(bf16[1,128,2048]{2,1,0:T(8,128)(2,1)S(1)} %collective-permute-done.3.g_ref) | copy-start | bytes 1572868
  46.8 22.5 %collective-permute-start.4 = (bf16[1,128,2048]{2,1,0:T(8,128)(2,1)S(1)}, bf16[1,128,2048]{2,1,0:T(8,128)(2,1)S(1)}, u32[]{:S(2)}, u32[]{:S(2)}) collective-permute-start(bf16[1,128,2048]{2,1,0:T(8,128)(2,1)S(1)} %collective-permute-done.3.g_ref), channel_id=1, source_target_pairs={{0,1},{1,2},{2,3},{3,0},{4,5},{5,6},{6,7},{7,4},{8,9},{9,10},{10,1... | collective-permute-start | bytes 1572872 | tf_op jit(solution)/shard_map/ppermute | solution.py:22
  58.0 22.5 %collective-permute-start.7 = (bf16[1,128,2048]{2,1,0:T(8,128)(2,1)S(1)}, bf16[1,128,2048]{2,1,0:T(8,128)(2,1)S(1)}, u32[]{:S(2)}, u32[]{:S(2)}) collective-permute-start(bf16[1,128,2048]{2,1,0:T(8,128)(2,1)S(1)} %collective-permute-done.5.q_ref), channel_id=1, source_target_pairs={{0,1},{1,2},{2,3},{3,0},{4,5},{5,6},{6,7},{7,4},{8,9},{9,10},{10,1... | collective-permute-start | bytes 1572872 | tf_op jit(solution)/shard_map/ppermute | solution.py:22
  69.2 20.7 %collective-permute-start.6 = (bf16[1,128,2048]{2,1,0:T(8,128)(2,1)S(1)}, bf16[1,128,2048]{2,1,0:T(8,128)(2,1)S(1)}, u32[]{:S(2)}, u32[]{:S(2)}) collective-permute-start(bf16[1,128,2048]{2,1,0:T(8,128)(2,1)S(1)} %collective-permute-done.4.g_ref), channel_id=1, source_target_pairs={{0,1},{1,2},{2,3},{3,0},{4,5},{5,6},{6,7},{7,4},{8,9},{9,10},{10,1... | collective-permute-start | bytes 1572872 | tf_op jit(solution)/shard_map/ppermute | solution.py:22
  92.1 3.7 %collective-permute-start.10 = (f32[2,4,2,8,128]{4,3,2,1,0:T(8,128)S(1)}, f32[2,4,2,8,128]{4,3,2,1,0:T(8,128)S(1)}, u32[]{:S(2)}, u32[]{:S(2)}) collective-permute-start(f32[2,4,2,8,128]{4,3,2,1,0:T(8,128)S(1)} %pad_maximum_fusion.1), channel_id=1, source_target_pairs={{0,3},{1,0},{2,1},{3,2},{4,7},{5,4},{6,5},{7,6},{8,11},{9,8},{10,9... | collective-permute-start | bytes 196616 | tf_op jit(solution)/shard_map/ppermute | solution.py:22
  93.9 7.2 %collective-permute-start.9 = (f32[2,4,2,8,128]{4,3,2,1,0:T(8,128)S(1)}, f32[2,4,2,8,128]{4,3,2,1,0:T(8,128)S(1)}, u32[]{:S(2)}, u32[]{:S(2)}) collective-permute-start(f32[2,4,2,8,128]{4,3,2,1,0:T(8,128)S(1)} %pad_maximum_fusion.1), channel_id=1, source_target_pairs={{0,2},{1,3},{2,0},{3,1},{4,6},{5,7},{6,4},{7,5},{8,10},{9,11},{10,... | collective-permute-start | bytes 196616 | tf_op jit(solution)/shard_map/ppermute | solution.py:22
  93.9 7.2 %collective-permute-start.8 = (f32[2,4,2,8,128]{4,3,2,1,0:T(8,128)S(1)}, f32[2,4,2,8,128]{4,3,2,1,0:T(8,128)S(1)}, u32[]{:S(2)}, u32[]{:S(2)}) collective-permute-start(f32[2,4,2,8,128]{4,3,2,1,0:T(8,128)S(1)} %pad_maximum_fusion.1), channel_id=1, source_target_pairs={{0,1},{1,2},{2,3},{3,0},{4,5},{5,6},{6,7},{7,4},{8,9},{9,10},{10,1... | collective-permute-start | bytes 196616 | tf_op jit(solution)/shard_map/ppermute | solution.py:22
  101.2 15.1 %collective-permute-start.13 = (bf16[128,2048]{1,0:T(8,128)(2,1)}, bf16[128,2048]{1,0:T(8,128)(2,1)S(1)}, u32[]{:S(2)}, u32[]{:S(2)}) collective-permute-start(bf16[128,2048]{1,0:T(8,128)(2,1)} %copy-done.11), channel_id=1, source_target_pairs={{0,1},{1,2},{2,3},{3,0},{4,5},{5,6},{6,7},{7,4},{8,9},{9,10},{10,1... | collective-permute-start | bytes 1572872 | tf_op jit(solution)/shard_map/ppermute | solution.py:22
  101.4 7.7 %collective-permute-start.12 = (f32[2,4,2,8,128]{4,3,2,1,0:T(8,128)S(1)}, f32[2,4,2,8,128]{4,3,2,1,0:T(8,128)S(1)}, u32[]{:S(2)}, u32[]{:S(2)}) collective-permute-start(f32[2,4,2,8,128]{4,3,2,1,0:T(8,128)S(1)} %get-tuple-element.68), channel_id=1, source_target_pairs={{4,0},{8,4},{12,8},{16,12},{20,16},{24,20},{28,24},{5,1},{9,5},{13... | collective-permute-start | bytes 196616 | tf_op jit(solution)/shard_map/ppermute | solution.py:27
  103.7 6.4 %collective-permute-start.11 = (f32[2,4,2,8,128]{4,3,2,1,0:T(8,128)S(1)}, f32[2,4,2,8,128]{4,3,2,1,0:T(8,128)S(1)}, u32[]{:S(2)}, u32[]{:S(2)}) collective-permute-start(f32[2,4,2,8,128]{4,3,2,1,0:T(8,128)S(1)} %get-tuple-element.69), channel_id=1, source_target_pairs={{0,4},{4,8},{8,12},{12,16},{16,20},{20,24},{24,28},{1,5},{5,9},{9,... | collective-permute-start | bytes 196616 | tf_op jit(solution)/shard_map/ppermute | solution.py:27
  117.8 14.0 %collective-permute-start.14 = (bf16[128,2048]{1,0:T(8,128)(2,1)S(1)}, bf16[128,2048]{1,0:T(8,128)(2,1)S(1)}, u32[]{:S(2)}, u32[]{:S(2)}) collective-permute-start(bf16[128,2048]{1,0:T(8,128)(2,1)S(1)} %mix_group.3), channel_id=1, source_target_pairs={{0,1},{1,2},{2,3},{3,0},{4,5},{5,6},{6,7},{7,4},{8,9},{9,10},{10,1... | collective-permute-start | bytes 1572872 | tf_op jit(solution)/shard_map/ppermute | solution.py:22
  119.9 13.3 %copy-start.8 = (bf16[1,128,2048]{2,1,0:T(8,128)(2,1)S(1)}, bf16[1,128,2048]{2,1,0:T(8,128)(2,1)}, u32[]{:S(2)}) copy-start(bf16[1,128,2048]{2,1,0:T(8,128)(2,1)} %copy-done.7) | copy-start | bytes 1572868
  131.6 14.0 %collective-permute-start.17 = (bf16[128,2048]{1,0:T(8,128)(2,1)S(1)}, bf16[128,2048]{1,0:T(8,128)(2,1)S(1)}, u32[]{:S(2)}, u32[]{:S(2)}) collective-permute-start(bf16[128,2048]{1,0:T(8,128)(2,1)S(1)} %convert_element_type.59), channel_id=1, source_target_pairs={{0,1},{1,2},{2,3},{3,0},{4,5},{5,6},{6,7},{7,4},{8,9},{9,10},{10,1... | collective-permute-start | bytes 1572872 | tf_op jit(solution)/shard_map/ppermute | solution.py:22
  133.0 23.8 %collective-permute-start.15 = (bf16[128,2048]{1,0:T(8,128)(2,1)S(1)}, bf16[128,2048]{1,0:T(8,128)(2,1)S(1)}, u32[]{:S(2)}, u32[]{:S(2)}) collective-permute-start(bf16[128,2048]{1,0:T(8,128)(2,1)S(1)} %mix_group.4), channel_id=1, source_target_pairs={{0,1},{1,2},{2,3},{3,0},{4,5},{5,6},{6,7},{7,4},{8,9},{9,10},{10,1... | collective-permute-start | bytes 1572872 | tf_op jit(solution)/shard_map/ppermute | solution.py:22
  133.3 33.6 %copy-start.6 = (bf16[1,128,2048]{2,1,0:T(8,128)(2,1)S(1)}, bf16[1,128,2048]{2,1,0:T(8,128)(2,1)}, u32[]{:S(2)}) copy-start(bf16[1,128,2048]{2,1,0:T(8,128)(2,1)} %copy-done.5) | copy-start | bytes 1572868
  145.7 32.7 %collective-permute-start.18 = (bf16[128,2048]{1,0:T(8,128)(2,1)S(1)}, bf16[128,2048]{1,0:T(8,128)(2,1)S(1)}, u32[]{:S(2)}, u32[]{:S(2)}) collective-permute-start(bf16[128,2048]{1,0:T(8,128)(2,1)S(1)} %add_convert_fusion.2), channel_id=1, source_target_pairs={{0,1},{1,2},{2,3},{3,0},{4,5},{5,6},{6,7},{7,4},{8,9},{9,10},{10,1... | collective-permute-start | bytes 1572872 | tf_op jit(solution)/shard_map/ppermute | solution.py:22
  158.1 32.3 %collective-permute-start.16 = (bf16[128,2048]{1,0:T(8,128)(2,1)S(1)}, bf16[128,2048]{1,0:T(8,128)(2,1)S(1)}, u32[]{:S(2)}, u32[]{:S(2)}) collective-permute-start(bf16[128,2048]{1,0:T(8,128)(2,1)S(1)} %fusion.2), channel_id=1, source_target_pairs={{0,4},{4,8},{8,12},{12,16},{16,20},{20,24},{24,28},{1,5},{5,9},{9,... | collective-permute-start | bytes 1572872 | tf_op jit(solution)/shard_map/ppermute | solution.py:27
  178.5 12.8 %collective-permute-start.19 = (bf16[128,2048]{1,0:T(8,128)(2,1)S(1)}, bf16[128,2048]{1,0:T(8,128)(2,1)S(1)}, u32[]{:S(2)}, u32[]{:S(2)}) collective-permute-start(bf16[128,2048]{1,0:T(8,128)(2,1)S(1)} %add_convert_fusion.1), channel_id=1, source_target_pairs={{0,1},{1,2},{2,3},{3,0},{4,5},{5,6},{6,7},{7,4},{8,9},{9,10},{10,1... | collective-permute-start | bytes 1572872 | tf_op jit(solution)/shard_map/ppermute | solution.py:22
  191.5 12.9 %collective-permute-start.20 = (bf16[128,2048]{1,0:T(8,128)(2,1)S(1)}, bf16[128,2048]{1,0:T(8,128)(2,1)S(1)}, u32[]{:S(2)}, u32[]{:S(2)}) collective-permute-start(bf16[128,2048]{1,0:T(8,128)(2,1)S(1)} %fusion.5), channel_id=1, source_target_pairs={{0,4},{4,8},{8,12},{12,16},{16,20},{20,24},{24,28},{1,5},{5,9},{9,... | collective-permute-start | bytes 1572872 | tf_op jit(solution)/shard_map/ppermute | solution.py:27
  (11 other events, 74.2 us)
